TPU v7x, 256 devices: a whole 4x4x8 slice. The times are simulated.
256 devices in a mesh: seq: 64 (over x, z, core), rep: 4 (over y).
Axes of the slice: x: 4, y: 4, z: 8, core: 2. Of those that a mesh axis runs over, the one named last changes fastest.
Arguments:
- feats: bfloat16 [262144, 256], P(('rep', 'seq')), parts along dimension 0, may hold values from -6 to 6
- hilbert_rank: int32 [262144], P(('rep', 'seq')), parts along dimension 0, may hold values from 0 to 65535, as said below
- patch_id: int32 [262144], P(('rep', 'seq')), parts along dimension 0, may hold values from 0 to 65535, as said below
- gain: float32 [256], replicated, may hold values from 0.5 to 1.5
- w_qkv: bfloat16 [256, 768], replicated, may hold values from -2.8125 to 2.8125, as said below
- w_out: bfloat16 [256, 256], replicated, may hold values from -1.5 to 1.5
- d_mixed: bfloat16 [262144, 256], P(('rep', 'seq')), parts along dimension 0, may hold values from -6 to 6
Outputs:
- mixed: bfloat16 [262144, 256], P(('rep', 'seq')), parts along dimension 0
- d_feats: bfloat16 [262144, 256], P(('rep', 'seq')), parts along dimension 0
- g_qkv: float32 [1024, 768], P('rep'), parts along dimension 0
- g_out: float32 [1024, 256], P('rep'), parts along dimension 0
- g_gain: float32 [1024], P('rep'), parts along dimension 0
There are 4 independent parts, one for each index of `rep`. A program takes and returns all parts, laid end to end along the dimension named above; an argument that names none is the same for every part. Nothing has to cross between parts.
Inputs may be any that keep to these rules, and one draw needn't show every extreme that they name: A permutation of the points. The owner of a point is hilbert_rank // 1024; of the points of one device at most 4 have any one other device as owner, and in every draw some device sends exactly 4 to some other. `patch_id`: the Hilbert index of the last point of the point's patch, so it never falls along the Hilbert order; patches are the aligned tiles of 1024 points, except that a tile in which a pooled cloud ends is split there into two patches; every patch lies inside one tile, and in every draw some patch fills a whole tile. `w_qkv`: dense real-valued projection.
All inputs are finite; a program needn't handle non-finite values.
Results may differ from a plain program's by a relative error of at most 0.025.
The roundings to bfloat16 on the way count: a program that leaves them out, or rounds other values in their place, can miss the bound.
Values may be sent and summed in bfloat16 or wider, within the bound.
A program may use at most 64 MiB of HBM per device.

v0:
```python
import jax
import jax.numpy as jnp
from jax import lax
from jax.sharding import PartitionSpec as P

HDIM = 16
PATCH = 1024
CAP = 4


eps = 1e-05


def layer_norm(rows):
    wide = rows.astype(jnp.float32)
    center = jnp.mean(wide, axis=1, keepdims=True)
    centred = wide - center
    recip = lax.rsqrt(jnp.mean(centred * centred, axis=1, keepdims=True) + eps)
    return (centred * recip, recip)


def head_attention(pieces, same, scale):
    query, keys, values, upper = pieces
    scores = jnp.dot(query, keys.T, preferred_element_type=jnp.float32) * scale
    scores = jnp.where(same, scores, -1e30)
    top = jnp.max(scores, axis=1, keepdims=True)
    expo = jnp.exp(scores - top)
    probs = expo / jnp.sum(expo, axis=1, keepdims=True)
    probs_low = probs.astype(jnp.bfloat16)
    attended = jnp.dot(probs_low, values, preferred_element_type=jnp.float32)
    grad_probs = jnp.dot(upper, values.T, preferred_element_type=jnp.float32)
    delta = jnp.sum(probs * grad_probs, axis=1, keepdims=True)
    grad_scores = (probs * (grad_probs - delta) * scale).astype(jnp.bfloat16)
    grad_query = jnp.dot(grad_scores, keys, preferred_element_type=jnp.float32)
    grad_keys = jnp.dot(grad_scores.T, query, preferred_element_type=jnp.float32)
    grad_values = jnp.dot(probs_low.T, upper, preferred_element_type=jnp.float32)
    return (attended, grad_query, grad_keys, grad_values)


def tile_attention(qkv_tile, labels, upstream):
    count = qkv_tile.shape[0]
    width = qkv_tile.shape[1] // 3
    heads = width // HDIM
    scale = HDIM ** (-0.5)

    def split_heads(block):
        return block.reshape(count, heads, HDIM).transpose(1, 0, 2)

    def join_heads(block):
        return block.transpose(1, 0, 2).reshape(count, width)

    query = split_heads(qkv_tile[:, :width])
    keys = split_heads(qkv_tile[:, width : 2 * width])
    values = split_heads(qkv_tile[:, 2 * width :])
    upper = split_heads(upstream)
    same = labels[:, None] == labels[None, :]
    attended, grad_query, grad_keys, grad_values = lax.map(
        lambda pieces: head_attention(pieces, same, scale), (query, keys, values, upper)
    )
    attended = join_heads(attended).astype(jnp.bfloat16)
    grad_qkv = jnp.concatenate(
        [join_heads(grad_query), join_heads(grad_keys), join_heads(grad_values)], axis=1
    ).astype(jnp.bfloat16)
    return (attended, grad_qkv)


def pack_rows(rows, target, slot, peers):
    empty = jnp.zeros((peers, CAP, rows.shape[1]), rows.dtype)
    return empty.at[target, slot].set(rows, mode="drop")


def settle(own_rows, arrived, positions, count):
    values = jnp.concatenate([own_rows, arrived.reshape(-1, arrived.shape[-1])], axis=0)
    empty = jnp.zeros((count, own_rows.shape[1]), own_rows.dtype)
    return empty.at[positions].set(values, mode="drop")


def norm_backward(grad_qkv, normed, normed_low, recip, gain, w_qkv, upstream):
    grad_normed = jnp.dot(grad_qkv, w_qkv.T, preferred_element_type=jnp.float32)
    g_qkv = jnp.dot(normed_low.T, grad_qkv, preferred_element_type=jnp.float32)
    g_gain = jnp.sum(grad_normed * normed, axis=0)
    scaled = grad_normed * gain
    d_norm = recip * (
        scaled
        - jnp.mean(scaled, axis=1, keepdims=True)
        - normed * jnp.mean(scaled * normed, axis=1, keepdims=True)
    )
    d_rows = (upstream.astype(jnp.float32) + d_norm).astype(jnp.bfloat16)
    return (d_rows, g_qkv, g_gain)


def on_device(feats, hilbert_rank, patch_id, gain, w_qkv, w_out, d_mixed):
    count = feats.shape[0]
    width = feats.shape[1]
    peers = lax.axis_size("seq")
    me = lax.axis_index("seq")
    owner = hilbert_rank // count
    onehot = (owner[:, None] == jnp.arange(peers, dtype=jnp.int32)[None, :]).astype(jnp.int32)
    slot = jnp.sum(jnp.cumsum(onehot, axis=0) * onehot, axis=1) - 1
    local = owner == me
    target = jnp.where(local, peers, owner)
    here = jnp.where(local, hilbert_rank - me * count, count)
    here_safe = jnp.where(local, here, 0)
    owner_safe = jnp.where(local, 0, owner)
    slot_safe = jnp.where(local, 0, slot)
    rank_slots = (
        jnp.full((peers, CAP), -1, jnp.int32).at[target, slot].set(hilbert_rank, mode="drop")
    )
    grad_att = jnp.dot(d_mixed, w_out.T, preferred_element_type=jnp.float32).astype(jnp.bfloat16)
    arrived, arrived_rank = (
        lax.all_to_all(
            pack_rows(feats, target, slot, peers), "seq", split_axis=0, concat_axis=0, tiled=True
        ),
        lax.all_to_all(rank_slots, "seq", split_axis=0, concat_axis=0, tiled=True),
    )
    positions = jnp.concatenate(
        [here, jnp.where(arrived_rank >= 0, arrived_rank - me * count, count).reshape(-1)]
    )
    hilbert = settle(feats, arrived, positions, count)
    normed, recip = layer_norm(hilbert)
    normed_low = (normed * gain).astype(jnp.bfloat16)
    qkv = jnp.dot(normed_low, w_qkv, preferred_element_type=jnp.float32).astype(jnp.bfloat16)
    tiles = count // PATCH
    attended, grad_qkv = lax.map(
        lambda pieces: tile_attention(pieces[0], pieces[1], pieces[2]),
        (
            qkv.reshape(tiles, PATCH, 3 * width),
            patch_id.reshape(tiles, PATCH),
            grad_att.reshape(tiles, PATCH, width),
        ),
    )
    attended = attended.reshape(count, width)
    grad_qkv = grad_qkv.reshape(count, 3 * width)
    mixed = (
        hilbert.astype(jnp.float32) + jnp.dot(attended, w_out, preferred_element_type=jnp.float32)
    ).astype(jnp.bfloat16)
    g_out = jnp.dot(attended.T, d_mixed, preferred_element_type=jnp.float32)
    back_index = jnp.where(arrived_rank >= 0, arrived_rank - me * count, 0)
    d_rows, g_qkv, g_gain = norm_backward(grad_qkv, normed, normed_low, recip, gain, w_qkv, d_mixed)
    returned = lax.all_to_all(d_rows[back_index], "seq", split_axis=0, concat_axis=0, tiled=True)
    d_feats = jnp.where(local[:, None], d_rows[here_safe], returned[owner_safe, slot_safe])
    g_qkv, g_out, g_gain = lax.psum((g_qkv, g_out, g_gain), "seq")
    return (mixed, d_feats, g_qkv, g_out, g_gain)


def solution(mesh):
    return jax.shard_map(
        on_device,
        mesh=mesh,
        in_specs=(
            P(("rep", "seq"), None),
            P(("rep", "seq")),
            P(("rep", "seq")),
            P(),
            P(),
            P(),
            P(("rep", "seq"), None),
        ),
        out_specs=(
            P(("rep", "seq"), None),
            P(("rep", "seq"), None),
            P("rep", None),
            P("rep", None),
            P("rep"),
        ),
        check_vma=False,
    )
```

profile of v0, /device:TPU:1, one launch (start us, length us, event | category | flops | bytes accessed | tf_op | source)
XLA Modules:
  0.0 606.4 jit_solution(6448323570177489621)
XLA Ops:
  8.7 18.0 %reduce-window.6 = s32[64,8,128]{2,1,0:T(8,128)S(1)} reduce-window(s32[64,8,128]{2,1,0:T(8,128)S(1)} %fusion.61, s32[]{:T(128)} %copy.50), window={size=1x1x128 pad=0_0x0_0x127_0}, to_apply=%region_0.1 | reduce-window | flops 8323072 | bytes 524292 | tf_op jit(solution)/shard_map/reduce-window
  30.9 4.5 scatter_custom_fusion.1
  36.1 13.0 %all-to-all-start = ((s32[64,1,4]{2,1,0:T(1,128)}), s32[64,1,4]{2,1,0:T(1,128)S(1)}, u32[]{:S(2)}, u32[]{:S(2)}) async-start(s32[64,1,4]{2,1,0:T(1,128)} %copy.22), calls=%async_computation | async-start | bytes 65536 | tf_op jit(solution)/shard_map/all_to_all | solution.py:114
  50.6 5.3 scatter_custom_fusion.2
  56.6 1.8 all-to-all-done
  58.4 8.6 %all-to-all-start.1 = ((bf16[64,4,256]{2,1,0:T(4,128)(2,1)}), bf16[64,4,256]{2,1,0:T(4,128)(2,1)S(1)}, u32[]{:S(2)}, u32[]{:S(2)}) async-start(bf16[64,4,256]{2,1,0:T(4,128)(2,1)} %reshape.266), calls=%async_computation.1 | async-start | bytes 262144 | tf_op jit(solution)/shard_map/all_to_all | solution.py:111
  67.3 10.0 %all-to-all-done.1 = bf16[64,4,256]{2,1,0:T(4,128)(2,1)S(1)} async-done(((bf16[64,4,256]{2,1,0:T(4,128)(2,1)}), bf16[64,4,256]{2,1,0:T(4,128)(2,1)S(1)}, u32[]{:S(2)}, u32[]{:S(2)}) %all-to-all-start.1) | async-done | bytes 131104 | tf_op jit(solution)/shard_map/all_to_all | solution.py:111
  77.3 9.5 %scatter_custom_fusion = bf16[1024,256]{1,0:T(8,128)(2,1)S(1)} fusion(s32[1280]{0:T(1024)S(1)} %fusion.65, bf16[256,256]{1,0:T(8,128)(2,1)S(1)} %reshape.251, bf16[]{:T(256)} %constant.130, bf16[1024,256]{1,0:T(8,128)(2,1)S(1)} %copy-done.3, bf16[]{:T(256)} %constant.84.clone.1), kind=kCustom, calls=%fused_computation.70 | custom fusion | flops 1310720 | bytes 1179652 | tf_op jit(solution)/shard_map/scatter | solution.py:75
  88.0 1.6 convolution_convert_fusion
  89.7 171.4 %while.28 = (s32[]{:T(128)}, bf16[16,1024,16]{1,2,0:T(8,128)(2,1)S(1)}, bf16[16,1024,16]{1,2,0:T(8,128)(2,1)}, bf16[16,1024,16]{1,2,0:T(8,128)(2,1)}, bf16[16,10...) while((s32[]{:T(128)}, ...), condition=%wide.region_12.13_spmd.clone, body=%wide.region_8.12_spmd.clone.sunk | while | flops 240120832 | bytes 40470644 | solution.py:57
  91.6 1.8 fusion.120
  94.7 1.5 multiply_reduce_fusion.5
  96.3 1.9 multiply_convert_fusion.2
  102.4 1.9 fusion.120
  105.4 1.5 multiply_reduce_fusion.5
  107.0 1.9 multiply_convert_fusion.2
  113.1 1.8 fusion.120
  116.2 1.5 multiply_reduce_fusion.5
  117.7 1.9 multiply_convert_fusion.2
  123.8 1.9 fusion.120
  126.9 1.5 multiply_reduce_fusion.5
  128.4 1.9 multiply_convert_fusion.2
  134.5 1.8 fusion.120
  139.1 1.9 multiply_convert_fusion.2
  145.2 1.9 fusion.120
  148.3 1.5 multiply_reduce_fusion.5
  149.8 1.9 multiply_convert_fusion.2
  155.9 1.8 fusion.120
  159.0 1.5 multiply_reduce_fusion.5
  160.5 1.9 multiply_convert_fusion.2
  166.6 1.9 fusion.120
  169.7 1.5 multiply_reduce_fusion.5
  171.3 1.9 multiply_convert_fusion.2
  177.3 1.8 fusion.120
  182.0 1.9 multiply_convert_fusion.2
  188.0 1.9 fusion.120
  192.7 1.9 multiply_convert_fusion.2
  198.7 1.9 fusion.120
  201.9 1.5 multiply_reduce_fusion.5
  203.4 1.9 multiply_convert_fusion.2
  209.5 1.9 fusion.120
  214.1 1.9 multiply_convert_fusion.2
  220.2 1.8 fusion.120
  223.3 1.5 multiply_reduce_fusion.5
  224.8 1.9 multiply_convert_fusion.2
  230.9 1.8 fusion.120
  234.0 1.5 multiply_reduce_fusion.5
  235.5 1.9 multiply_convert_fusion.2
  241.6 1.8 fusion.120
  244.7 1.5 multiply_reduce_fusion.5
  246.2 1.9 multiply_convert_fusion.2
  252.3 1.8 fusion.120
  256.9 1.9 multiply_convert_fusion.2
  261.2 3.3 fusion.56
  264.5 2.0 fusion.50
  267.5 124.6 %psum.23 = f32[256]{0:T(256)} all-reduce(f32[256]{0:T(256)S(1)} %get-tuple-element.105), channel_id=1, replica_groups=mesh['seq'=64,'rep'=4] {'seq'}, use_global_device_ids=true, to_apply=%region_18.19 | all-reduce | flops 256 | bytes 2048 | tf_op jit(solution)/shard_map/psum | solution.py:142
  392.1 1.9 fusion.49
  395.1 4.4 gather_fusion
  400.3 5.9 all-to-all-start.2
  408.0 8.6 %all-to-all-done.2 = bf16[64,4,256]{2,1,0:T(4,128)(2,1)S(1)} async-done(((bf16[64,4,256]{2,1,0:T(4,128)(2,1)}), bf16[64,4,256]{2,1,0:T(4,128)(2,1)S(1)}, u32[]{:S(2)}, u32[]{:S(2)}) %all-to-all-start.2) | async-done | bytes 131104 | tf_op jit(solution)/shard_map/all_to_all | solution.py:140
  416.6 5.8 gather_fusion.2
  423.4 172.4 %all-reduce.3.cloned.1.call-done = (f32[256,768]{1,0:T(8,128)}, f32[256,256]{1,0:T(8,128)}) async-done(((f32[256,768]{1,0:T(8,128)}, f32[256,256]{1,0:T(8,128)}), (f32[256,768]{1,0:T(8,128)}, f32[256,256]{1,0:T(8,128)})) %all-reduce.3.cloned.1.call-update) | async-done | bytes 1048592 | tf_op jit(solution)/shard_map/psum | solution.py:142
  595.8 2.1 copy.51
  597.9 1.7 copy.52
  (153 shorter events, 109.9 us)
Async XLA Ops:
  7.2 80.9 %copy-start = (bf16[256,768]{1,0:T(8,128)(2,1)S(1)}, bf16[256,768]{1,0:T(8,128)(2,1)}, u32[]{:S(2)}) copy-start(bf16[256,768]{1,0:T(8,128)(2,1)} %param.13) | copy-start | bytes 1179652
  7.2 70.2 %copy-start.3 = (bf16[1024,256]{1,0:T(8,128)(2,1)S(1)}, bf16[1024,256]{1,0:T(8,128)(2,1)}, u32[]{:S(2)}) copy-start(bf16[1024,256]{1,0:T(8,128)(2,1)} %param.9) | copy-start | bytes 1572868
  7.2 80.8 %copy-start.7 = (f32[256]{0:T(256)S(1)}, f32[256]{0:T(256)}, u32[]{:S(2)}) copy-start(f32[256]{0:T(256)} %param.12) | copy-start | bytes 3076
  28.0 22.5 %copy-start.5 = (pred[1024]{0:T(1024)(128)(4,1)}, pred[1024]{0:T(1024)(128)(4,1)S(1)}, u32[]{:S(2)}) copy-start(pred[1024]{0:T(1024)(128)(4,1)S(1)} %get-tuple-element.133) | copy-start | bytes 3076
  36.1 22.2 %all-to-all-start = ((s32[64,1,4]{2,1,0:T(1,128)}), s32[64,1,4]{2,1,0:T(1,128)S(1)}, u32[]{:S(2)}, u32[]{:S(2)}) async-start(s32[64,1,4]{2,1,0:T(1,128)} %copy.22), calls=%async_computation | async-start | bytes 65536 | tf_op jit(solution)/shard_map/all_to_all | solution.py:114
  58.4 18.9 %all-to-all-start.1 = ((bf16[64,4,256]{2,1,0:T(4,128)(2,1)}), bf16[64,4,256]{2,1,0:T(4,128)(2,1)S(1)}, u32[]{:S(2)}, u32[]{:S(2)}) async-start(bf16[64,4,256]{2,1,0:T(4,128)(2,1)} %reshape.266), calls=%async_computation.1 | async-start | bytes 262144 | tf_op jit(solution)/shard_map/all_to_all | solution.py:111
  67.1 22.7 %copy-start.2 = (s32[1024]{0:T(1024)S(1)}, s32[1024]{0:T(1024)}, u32[]{:S(2)}) copy-start(s32[1024]{0:T(1024)} %param.11) | copy-start | bytes 12292
  261.1 3.4 copy-start.8
  261.1 3.4 copy-start.9
  261.1 3.4 copy-start.10
  261.1 3.4 copy-start.11
  264.5 2.0 copy-start.1
  394.0 12.9 %copy-start.4 = (bf16[256,256]{1,0:T(8,128)(2,1)S(1)}, bf16[256,256]{1,0:T(8,128)(2,1)}, u32[]{:S(2)}) copy-start(bf16[256,256]{1,0:T(8,128)(2,1)} %param.14) | copy-start | bytes 393220
  400.3 22.1 %copy-start.6 = (pred[1024]{0:T(1024)(128)(4,1)S(1)}, pred[1024]{0:T(1024)(128)(4,1)}, u32[]{:S(2)}) copy-start(pred[1024]{0:T(1024)(128)(4,1)} %copy-done.5) | copy-start | bytes 3076
  400.3 16.3 %all-to-all-start.2 = ((bf16[64,4,256]{2,1,0:T(4,128)(2,1)}), bf16[64,4,256]{2,1,0:T(4,128)(2,1)S(1)}, u32[]{:S(2)}, u32[]{:S(2)}) async-start(bf16[64,4,256]{2,1,0:T(4,128)(2,1)} %reshape.276), calls=%async_computation.2 | async-start | bytes 262144 | tf_op jit(solution)/shard_map/all_to_all | solution.py:140
  406.1 189.7 %all-reduce.3.cloned.1.call-start = ((), (), s32[]{:S(2)}) async-start(), calls=%async_computation.3 | async-start | bytes 2097152 | tf_op jit(solution)/shard_map/psum | solution.py:142
Sparse Core Ops, SparseCore 0:
  411.0 184.7 all-reduce.2
where the time goes:
time: 608 us; the launch traced here: 606 us
  waiting for transfers between devices  193 us (32%)
  matrix products  134 us (22%)
  blocking collectives  125 us (21%)
  other arithmetic  83.8 us (14%)
  local copies, waits for them, and re-layouts  27.8 us (5%)
  starting transfers between devices  27.5 us (5%)
  between operations  14.4 us (2%)
    psum x1, waiting for transfers between devices, on_device(): g_qkv, g_out, g_gain = lax.psum((g_qkv, g_out, g_gain), 'seq')  172 us
    psum x1, blocking collectives, on_device(): g_qkv, g_out, g_gain = lax.psum((g_qkv, g_out, g_gain), 'seq')  125 us
    convert_element_type x16, other arithmetic, head_attention(): grad_scores = (probs * (grad_probs - delta) * scale).astype(jnp.bfloat16)  30.4 us
    dot_general x16, matrix products, head_attention(): jnp.dot(probs_low.T, upper, preferred_element_type=jnp.float32)  29.6 us
    dot_general x16, matrix products, head_attention(): grad_probs = jnp.dot(upper, values.T, preferred_element_type=jnp.float32)  24.6 us
    dot_general x16, matrix products, head_attention(): jnp.dot(grad_scores.T, query, preferred_element_type=jnp.float32)  20.5 us
    dot_general x16, matrix products, head_attention(): attended = jnp.dot(probs_low, values, preferred_element_type=jnp.float32)  19.9 us
    another operation x7, other arithmetic  18.2 us
  transfers between devices with their start and end apart: 4, of which 4 were waited for; matrix products, arithmetic and copies ran while one was open for 3% of the time, Pallas kernels for 0%

commit v1 on v0

v1 whole, which is shorter than its diff:
```python
import functools

import jax
import jax.numpy as jnp
from jax import lax
from jax.experimental import pallas as pl
from jax.experimental.pallas import tpu as pltpu
from jax.sharding import PartitionSpec as P

F = jnp.float32
B = jnp.bfloat16
I = jnp.int32

N = 1024
C = 256
HDIM = 16
HEADS = C // HDIM
PEERS = 64
CAP = 4
ROWS = 16
CHIPS = 32
PIECE = 32
EPS = 1e-05
MASKED = 1e30
VMEM = 56 << 20

ANYWHERE = pl.BlockSpec(memory_space=pltpu.VMEM)


def dg(a, b, ca, cb):
    return lax.dot_general(a, b, (((ca,), (cb,)), ((), ())), preferred_element_type=F)


def iota(shape, dim):
    return lax.broadcasted_iota(I, shape, dim)


def greet():
    me = lax.axis_index("seq")
    barrier = pltpu.get_barrier_semaphore()

    def signal(step, carry):
        peer = lax.rem(me + step, PEERS)
        pl.semaphore_signal(
            barrier, inc=1, device_id={"seq": peer}, device_id_type=pl.DeviceIdType.MESH
        )
        return carry

    lax.fori_loop(1, PEERS, signal, 0)


def met():
    pl.semaphore_wait(pltpu.get_barrier_semaphore(), PEERS - 1)


def remote(src, dst, send_sem, recv_sem, peer):
    return pltpu.make_async_remote_copy(
        src_ref=src,
        dst_ref=dst,
        send_sem=send_sem,
        recv_sem=recv_sem,
        device_id={"seq": peer},
        device_id_type=pl.DeviceIdType.MESH,
    )


def await_bytes(ref, sem):
    pltpu.make_async_copy(ref, ref, sem).wait()


def exchange(src, dst, send_sem, recv_sem):
    me = lax.axis_index("seq")
    mine = pl.ds(pl.multiple_of(me * ROWS, ROWS), ROWS)

    def send(step, carry):
        peer = lax.rem(me + step, PEERS)
        theirs = pl.ds(pl.multiple_of(peer * ROWS, ROWS), ROWS)
        remote(src.at[theirs], dst.at[mine], send_sem, recv_sem, peer).start()
        return carry

    lax.fori_loop(1, PEERS, send, 0)


def await_exchange(ref, sem):
    await_bytes(ref.at[pl.ds(0, (PEERS - 1) * ROWS)], sem)


def slot_rows(code):
    r = iota((PEERS * ROWS, 1), 0)
    t = r % ROWS
    wanted = jnp.where(t < 3 * CAP, (r // ROWS) * CAP + t % CAP, -2)
    return wanted == code


def pack_kernel(rank_ref, feats_ref, code_ref, got_ref, send, send_sem, recv_sem):
    greet()
    me = lax.axis_index("seq")
    rank = rank_ref[...]
    owner = rank // N
    onehot = (iota((PEERS, N), 0) == owner).astype(F)
    upto = (iota((N, N), 0) <= iota((N, N), 1)).astype(F).astype(B)
    count = jnp.dot(onehot.astype(B), upto, preferred_element_type=F)
    slot = jnp.sum(count * onehot, axis=0, keepdims=True).astype(I) - 1
    code = jnp.where(owner == me, -1, owner * CAP + slot)
    code_ref[...] = code
    chosen = slot_rows(code).astype(F).astype(B)
    place = rank % N
    k = iota((128, N), 0)
    extra = jnp.where(k == 0, place // 32, jnp.where(k == 1, place % 32, jnp.where(k == 2, 1, 0)))
    rows = jnp.dot(chosen, feats_ref[...], preferred_element_type=F)
    places = dg(chosen, extra.astype(F).astype(B), 1, 1)
    t = iota((PEERS * ROWS, 128), 0) % ROWS
    block = jnp.where(t < CAP, rows[:, :128], jnp.where(t < 2 * CAP, rows[:, 128:], places))
    send[...] = block.astype(B)
    got_ref[pl.ds(pl.multiple_of(me * ROWS, ROWS), ROWS), :] = jnp.zeros((ROWS, 128), B)
    met()
    exchange(send, got_ref, send_sem, recv_sem)
    await_exchange(got_ref, recv_sem)
    await_exchange(send, send_sem)


def halves(block, t):
    zero = jnp.zeros_like(block)
    left = jnp.where(t < CAP, block, zero)
    right = jnp.where((t >= CAP) & (t < 2 * CAP), block, zero)
    return jnp.concatenate([left, right], axis=1)


def attention(q_ref, k_ref, v_ref, u_ref, group, att, gq, gk, gv):
    one = jnp.where(group > 0, 1.0, 0.0)
    pad = jnp.zeros((HDIM - 2, N), F)
    q_bias = jnp.concatenate([-MASKED * (1 - one), -MASKED * one, pad], 0).astype(B)
    k_bias = jnp.concatenate([one, 1 - one, pad], 0).astype(B)
    ones = jnp.concatenate([jnp.ones((1, N), F), jnp.zeros((HDIM - 1, N), F)], 0).astype(B)
    scale = HDIM ** (-0.5)

    def head(h, carry):
        rows = pl.ds(pl.multiple_of(h * HDIM, HDIM), HDIM)
        q, k, v, u = q_ref[rows, :], k_ref[rows, :], v_ref[rows, :], u_ref[rows, :]
        qx = jnp.concatenate([q * B(scale), q_bias], 0)
        kx = jnp.concatenate([k, k_bias], 0)
        vx = jnp.concatenate([v, ones], 0)
        scores = dg(kx, qx, 0, 0)
        expo = jnp.exp(scores - jnp.max(scores, axis=0, keepdims=True))
        low = expo.astype(B)
        total = jnp.dot(vx, low, preferred_element_type=F)
        recip = 1.0 / total[HDIM : HDIM + 1]
        attended = total[:HDIM] * recip
        wide = u.astype(F)
        delta = jnp.sum(wide * attended, axis=0, keepdims=True)
        grad_probs = dg(v, u, 0, 0)
        grad_scores = (expo * ((grad_probs - delta) * (recip * scale))).astype(B)
        att[rows, :] = attended.astype(B)
        gq[rows, :] = jnp.dot(k, grad_scores, preferred_element_type=F).astype(B)
        gk[rows, :] = dg(q, grad_scores, 1, 1).astype(B)
        gv[rows, :] = dg((wide * recip).astype(B), low, 1, 1).astype(B)
        return carry

    lax.fori_loop(0, HEADS, head, 0)


def layer_kernel(
    rank_ref, got_ref, feats_ref, patch_ref, gain_ref, w_qkv_ref, w_out_ref, d_mixed_ref,
    mixed_ref, local_ref, back_ref, grads_ref,
    hil, qkv, up, normed, low, att, gqkv, place,
):
    me = lax.axis_index("seq")
    rank = rank_ref[...]
    here = jnp.where(rank // N == me, rank % N, -1)
    got = got_ref[...]
    weight = iota((16, 128), 1)
    weight = jnp.where(weight == 0, 32.0, jnp.where(weight < 2, 1.0, 0.0)).astype(B)
    valid = jnp.where(iota((16, 128), 1) == 2, 1.0, 0.0).astype(B)
    lane = iota((1, N), 1) % ROWS
    at = dg(weight, got, 1, 1)[:1]
    real = dg(valid, got, 1, 1)[:1]
    at = jnp.where(real > 0.5, at, -1.0)
    at = jnp.where(lane < 2 * CAP, -1.0, jnp.where(lane < 3 * CAP, at, -1.0))
    at = jnp.broadcast_to(at, (8, N))
    left = pltpu.roll(at, N - 2 * CAP, 1)[:1]
    right = pltpu.roll(at, N - CAP, 1)[:1]
    at = jnp.where(lane < CAP, left, jnp.where(lane < 2 * CAP, right, -1.0)).astype(I)
    place[...] = jnp.broadcast_to(at, (8, N))
    p = iota((N, 1), 0)
    t = iota((PEERS * ROWS, 128), 0) % ROWS
    stay = (p == here).astype(F).astype(B)
    come = (p == at).astype(F).astype(B)
    rows = jnp.dot(stay, feats_ref[...], preferred_element_type=F)
    rows += jnp.dot(come, halves(got, t), preferred_element_type=F)
    hil[...] = rows.astype(B)

    gain = jnp.broadcast_to(gain_ref[...], (8, C)).T[:, :1]
    wide = rows.T
    centred = wide - jnp.mean(wide, axis=0, keepdims=True)
    recip = lax.rsqrt(jnp.mean(centred * centred, axis=0, keepdims=True) + EPS)
    normed[...] = centred * recip
    low[...] = (normed[...] * gain).astype(B)
    qkv[...] = dg(w_qkv_ref[...], low[...], 0, 0).astype(B)
    up[...] = dg(w_out_ref[...], d_mixed_ref[...], 1, 1).astype(B)

    patch = patch_ref[...]
    attention(
        qkv.at[:C], qkv.at[C : 2 * C], qkv.at[2 * C :], up,
        (patch == patch[:, :1]).astype(F),
        att, gqkv.at[:C], gqkv.at[C : 2 * C], gqkv.at[2 * C :],
    )

    mixed_ref[...] = (hil[...].astype(F) + dg(att[...], w_out_ref[...], 0, 0)).astype(B)
    g_out = jnp.dot(att[...], d_mixed_ref[...], preferred_element_type=F)
    g_qkv = dg(low[...], gqkv[...], 1, 1)
    for j in range(6):
        grads_ref[j * C : (j + 1) * C, :] = g_qkv[:, j * 128 : (j + 1) * 128]
    for j in range(2):
        grads_ref[(6 + j) * C : (7 + j) * C, :] = g_out[:, j * 128 : (j + 1) * 128]

    grad_normed = jnp.dot(w_qkv_ref[...], gqkv[...], preferred_element_type=F)
    scaled = grad_normed * gain
    d_norm = recip * (
        scaled
        - jnp.mean(scaled, axis=0, keepdims=True)
        - normed[...] * jnp.mean(scaled * normed[...], axis=0, keepdims=True)
    )
    d_rows = (d_mixed_ref[...].astype(F).T + d_norm).astype(B)
    stay = (p == here).astype(F).astype(B)
    come = (p == place[:1]).astype(F).astype(B)
    local_ref[...] = jnp.dot(d_rows, stay, preferred_element_type=F).astype(B)
    back = jnp.dot(d_rows, come, preferred_element_type=F)
    back = jnp.where(lane < CAP, back[:128], jnp.where(lane < 2 * CAP, back[128:], 0.0))
    back_ref[...] = back.T.astype(B)


def return_kernel(
    back_ref, grads_ref, ret_ref, sums_ref,
    half_send, half_got, piece_send, piece_got, done,
    row_sems, half_sems, piece_sems, done_sems, last_sems,
):
    greet()
    me = lax.axis_index("seq")
    core = lax.rem(me, 2)
    chip = me // 2
    other = 1 - core
    partner = chip * 2 + other
    half = CHIPS * PIECE

    half_send[...] = grads_ref[pl.ds(pl.multiple_of(other * half, half), half), :].astype(B)
    ret_ref[pl.ds(pl.multiple_of(me * ROWS, ROWS), ROWS), :] = jnp.zeros((ROWS, 128), B)
    met()
    swap = remote(half_send, half_got, half_sems.at[0], half_sems.at[1], partner)
    swap.start()
    exchange(back_ref, ret_ref, row_sems.at[0], row_sems.at[1])
    swap.wait()

    mine = grads_ref[pl.ds(pl.multiple_of(core * half, half), half), :]
    piece_send[...] = (mine + half_got[...].astype(F)).astype(B)
    own = pl.ds(pl.multiple_of(chip * PIECE, PIECE), PIECE)
    piece_got[own, :] = piece_send[own, :]

    def scatter(step, carry):
        to = lax.rem(chip + step, CHIPS)
        theirs = pl.ds(pl.multiple_of(to * PIECE, PIECE), PIECE)
        remote(
            piece_send.at[theirs], piece_got.at[own], piece_sems.at[0], piece_sems.at[1],
            to * 2 + core,
        ).start()
        return carry

    lax.fori_loop(1, CHIPS, scatter, 0)
    others = pl.ds(0, (CHIPS - 1) * PIECE)
    await_bytes(piece_got.at[others], piece_sems.at[1])
    total = piece_got[0:PIECE, :].astype(F)
    for j in range(1, CHIPS):
        total += piece_got[j * PIECE : (j + 1) * PIECE, :].astype(F)
    done[own, :] = total.astype(B)

    def gather(step, carry):
        to = lax.rem(chip + step, CHIPS)
        remote(
            done.at[own], done.at[own], done_sems.at[0], done_sems.at[1], to * 2 + core
        ).start()
        return carry

    lax.fori_loop(1, CHIPS, gather, 0)
    await_bytes(done.at[others], done_sems.at[1])
    here = pl.ds(pl.multiple_of(core * half, half), half)
    last = remote(done, sums_ref.at[here], last_sems.at[0], last_sems.at[1], partner)
    last.start()
    sums_ref[here, :] = done[...]
    await_exchange(ret_ref, row_sems.at[1])
    await_exchange(back_ref, row_sems.at[0])
    await_bytes(piece_send.at[others], piece_sems.at[0])
    await_bytes(done.at[others], done_sems.at[0])
    last.wait()


def finish_kernel(
    code_ref, ret_ref, local_ref, sums_ref, w_qkv_ref, gain_ref,
    d_feats_ref, g_qkv_ref, g_out_ref, g_gain_ref,
):
    t = iota((PEERS * ROWS, 128), 0) % ROWS
    chosen = slot_rows(code_ref[...]).astype(F).astype(B)
    d_feats = dg(halves(ret_ref[...], t), chosen, 0, 0) + local_ref[...].astype(F)
    d_feats_ref[...] = d_feats.T.astype(B)
    total = jnp.zeros((C, 128), F)
    for j in range(6):
        part = sums_ref[j * C : (j + 1) * C, :].astype(F)
        g_qkv_ref[:, j * 128 : (j + 1) * 128] = part
        total += part * w_qkv_ref[:, j * 128 : (j + 1) * 128].astype(F)
    for j in range(2):
        g_out_ref[:, j * 128 : (j + 1) * 128] = sums_ref[(6 + j) * C : (7 + j) * C, :].astype(F)
    g_gain_ref[...] = jnp.sum(total.T, axis=0, keepdims=True) / gain_ref[...]


def call(kernel, out_shapes, n_in, scratch=(), collective_id=None):
    params = dict(vmem_limit_bytes=VMEM)
    if collective_id is not None:
        params.update(collective_id=collective_id, has_side_effects=True)
    return pl.pallas_call(
        kernel,
        out_shape=[jax.ShapeDtypeStruct(s, d) for s, d in out_shapes],
        in_specs=[ANYWHERE] * n_in,
        out_specs=[ANYWHERE] * len(out_shapes),
        scratch_shapes=list(scratch),
        compiler_params=pltpu.CompilerParams(**params),
    )


def on_device(feats, hilbert_rank, patch_id, gain, w_qkv, w_out, d_mixed):
    rank = hilbert_rank.reshape(1, N)
    patch = patch_id.reshape(1, N)
    gain = gain.reshape(1, C)
    blocks = (PEERS * ROWS, 128)
    dma = pltpu.SemaphoreType.DMA
    code, got = call(
        pack_kernel, [((1, N), I), (blocks, B)], 2,
        [pltpu.VMEM(blocks, B), dma, dma], collective_id=0,
    )(rank, feats)
    mixed, local, back, grads = call(
        layer_kernel, [((N, C), B), ((C, N), B), (blocks, B), ((8 * C, 128), F)], 8,
        [
            pltpu.VMEM((N, C), B), pltpu.VMEM((3 * C, N), B), pltpu.VMEM((C, N), B),
            pltpu.VMEM((C, N), F), pltpu.VMEM((C, N), B), pltpu.VMEM((C, N), B),
            pltpu.VMEM((3 * C, N), B), pltpu.VMEM((8, N), I),
        ],
    )(rank, got, feats, patch, gain, w_qkv, w_out, d_mixed)
    half = (CHIPS * PIECE, 128)
    ret, sums = call(
        return_kernel, [(blocks, B), ((8 * C, 128), B)], 2,
        [pltpu.VMEM(half, B)] * 5 + [dma((2,))] * 5, collective_id=1,
    )(back, grads)
    d_feats, g_qkv, g_out, g_gain = call(
        finish_kernel, [((N, C), B), ((C, 3 * C), F), ((C, C), F), ((1, C), F)], 6
    )(code, ret, local, sums, w_qkv, gain)
    return (mixed, d_feats, g_qkv, g_out, g_gain.reshape(C))


def solution(mesh):
    return jax.shard_map(
        on_device,
        mesh=mesh,
        in_specs=(
            P(("rep", "seq"), None),
            P(("rep", "seq")),
            P(("rep", "seq")),
            P(),
            P(),
            P(),
            P(("rep", "seq"), None),
        ),
        out_specs=(
            P(("rep", "seq"), None),
            P(("rep", "seq"), None),
            P("rep", None),
            P("rep", None),
            P("rep"),
        ),
        check_vma=False,
    )
```

time: 608 us -> 123 us (0.20)
  waiting for transfers between devices: 193 us -> 0 us
  matrix products: 134 us -> 0 us
  blocking collectives: 125 us -> 0 us
  Pallas kernels: 0 us -> 122 us
  other arithmetic: 83.8 us -> 0 us
  local copies, waits for them, and re-layouts: 27.8 us -> 0 us
  starting transfers between devices: 27.5 us -> 0 us
  between operations: 14.4 us -> 0.65 us
    psum x1 -> x0, waiting for transfers between devices: 172 us -> none  [on_device(): g_qkv, g_out, g_gain = lax.psum((g_qkv, g_out, g_gain), 'seq')]
    dot_general x102 -> x0, matrix products: 134 us -> none  [the longest x16 29.6 us: head_attention(): jnp.dot(probs_low.T, upper, preferred_element_type=jnp.float32)]
    psum x1 -> x0, blocking collectives: 125 us -> none  [on_device(): g_qkv, g_out, g_gain = lax.psum((g_qkv, g_out, g_gain), 'seq')]
    pallas_call x0 -> x4, Pallas kernels: none -> 122 us  [the longest x1 63.8 us: on_device(): call(layer_kernel, [((N, C), B), ((C, N), B), (blocks, B), ((8 * C, 128),...]
    convert_element_type x18 -> x0, other arithmetic: 32.3 us -> none  [the longest x16 30.4 us: head_attention(): grad_scores = (probs * (grad_probs - delta) * scale).astype(jnp.bfloat16)]
    all_to_all x3 -> x0, starting transfers between devices: 27.4 us -> none  [the longest x1 13 us: on_device(): lax.all_to_all(rank_slots, 'seq', split_axis=0, concat_axis=0, tiled=True)]
    all_to_all x3 -> x0, waiting for transfers between devices: 20.3 us -> none  [the longest x1 9.95 us: on_device(): lax.all_to_all(pack_rows(feats, target, slot, peers), 'seq', split_axis=0...]
    another operation x7 -> x0, other arithmetic: 18.2 us -> none
  transfers between devices with their start and end apart: 4 -> 0, of which waited for: 4 -> 0; matrix products, arithmetic and copies ran while one was open for 3% -> 0% of each run, Pallas kernels for 0% -> 0%
where the time goes in v1:
time: 123 us; the launch traced here: 122 us
  Pallas kernels  122 us (99%)
    pallas_call x1, Pallas kernels, on_device(): call(layer_kernel, [((N, C), B), ((C, N), B), (blocks, B), ((8 * C, 128),...  63.8 us
    pallas_call x1, Pallas kernels, on_device(): call(return_kernel, [(blocks, B), ((8 * C, 128), B)], 2, [pltpu.VMEM(half...  34 us
    pallas_call x1, Pallas kernels, on_device(): call(pack_kernel, [((1, N), I), (blocks, B)], 2, [pltpu.VMEM(blocks, B),...  20.7 us
    pallas_call x1, Pallas kernels, on_device(): call(finish_kernel, [((N, C), B), ((C, 3 * C), F), ((C, C), F), ((1, C),...  3.37 us

profile of v1, /device:TPU:1, one launch (start us, length us, event | category | flops | bytes accessed | tf_op | source)
XLA Modules:
  0.0 122.5 jit_solution(471663065461376907)
XLA Ops:
  0.6 20.7 %shard_map.110 = (s32[1,1024]{1,0:T(1,128)}, bf16[1024,128]{1,0:T(8,128)(2,1)}) custom-call(s32[1,1024]{1,0:T(1,128)} %bitcast.4, bf16[1024,256]{1,0:T(8,128)(2,1)} %feats_ref.3), custom_call_target="tpu_custom_call" | custom-call | tf_op jit(solution)/shard_map/pallas_call | solution.py:333
  21.4 63.8 %shard_map.111 = (bf16[1024,256]{1,0:T(8,128)(2,1)}, bf16[256,1024]{1,0:T(8,128)(2,1)}, bf16[1024,128]{1,0:T(8,128)(2,1)}, f32[2048,128]{1,0:T(8,128)}) custom-call(s32[1,1024]{1,0:T(1,128)} %bitcast.5, bf16[1024,128]{1,0:T(8,128)(2,1)} %get-tuple-element.17.got_ref, bf16[1024,256]{1,0:T(8,128)(2,1)} %feats_ref.3, s32[1,1024]{1,0:T(1,128)} %bitcast.6, ...), custom_call_target="tpu_custom_call" | custom-call | tf_op jit(solution)/shard_map/pallas_call | solution.py:337
  85.1 34.0 %shard_map.112 = (bf16[1024,128]{1,0:T(8,128)(2,1)}, bf16[2048,128]{1,0:T(8,128)(2,1)}) custom-call(bf16[1024,128]{1,0:T(8,128)(2,1)} %get-tuple-element.20.back_ref, f32[2048,128]{1,0:T(8,128)} %get-tuple-element.21.grads_ref), custom_call_target="tpu_custom_call" | custom-call | tf_op jit(solution)/shard_map/pallas_call | solution.py:346
  119.1 3.4 %shard_map.113 = (bf16[1024,256]{1,0:T(8,128)(2,1)}, f32[256,768]{1,0:T(8,128)}, f32[256,256]{1,0:T(8,128)}, f32[1,256]{1,0:T(1,128)}) custom-call(s32[1,1024]{1,0:T(1,128)} %get-tuple-element.19.code_ref, bf16[1024,128]{1,0:T(8,128)(2,1)} %get-tuple-element.22.ret_ref, bf16[256,1024]{1,0:T(8,128)(2,1)} %get-tuple-element.23.local_ref, ...), custom_call_target="tpu_custom_call" | custom-call | tf_op jit(solution)/shard_map/pallas_call | solution.py:350

commit v2 on v1

v2 whole, which is shorter than its diff:
```python
import functools

import jax
import jax.numpy as jnp
from jax import lax
from jax.experimental import pallas as pl
from jax.experimental.pallas import tpu as pltpu
from jax.sharding import PartitionSpec as P

F = jnp.float32
B = jnp.bfloat16
I = jnp.int32

N = 1024
C = 256
HDIM = 16
HEADS = C // HDIM
PEERS = 64
CAP = 4
ROWS = 16
CHIPS = 32
GROUPS = 2
WIDE = C // GROUPS
PIECE = 16
HALF = CHIPS * PIECE
EPS = 1e-05
MASKED = 1e30
VMEM = 56 << 20

ANYWHERE = pl.BlockSpec(memory_space=pltpu.VMEM)


def dg(a, b, ca, cb):
    return lax.dot_general(a, b, (((ca,), (cb,)), ((), ())), preferred_element_type=F)


def iota(shape, dim):
    return lax.broadcasted_iota(I, shape, dim)


def greet():
    me = lax.axis_index("seq")
    barrier = pltpu.get_barrier_semaphore()

    def signal(step, carry):
        peer = lax.rem(me + step, PEERS)
        pl.semaphore_signal(
            barrier, inc=1, device_id={"seq": peer}, device_id_type=pl.DeviceIdType.MESH
        )
        return carry

    lax.fori_loop(1, PEERS, signal, 0)


def met():
    pl.semaphore_wait(pltpu.get_barrier_semaphore(), PEERS - 1)


def remote(src, dst, send_sem, recv_sem, peer):
    return pltpu.make_async_remote_copy(
        src_ref=src,
        dst_ref=dst,
        send_sem=send_sem,
        recv_sem=recv_sem,
        device_id={"seq": peer},
        device_id_type=pl.DeviceIdType.MESH,
    )


def await_bytes(ref, sem):
    pltpu.make_async_copy(ref, ref, sem).wait()


def exchange(src, dst, send_sem, recv_sem):
    me = lax.axis_index("seq")
    mine = pl.ds(pl.multiple_of(me * ROWS, ROWS), ROWS)

    def send(step, carry):
        peer = lax.rem(me + step, PEERS)
        theirs = pl.ds(pl.multiple_of(peer * ROWS, ROWS), ROWS)
        remote(src.at[theirs], dst.at[mine], send_sem, recv_sem, peer).start()
        return carry

    lax.fori_loop(1, PEERS, send, 0)


def await_exchange(ref, sem):
    await_bytes(ref.at[pl.ds(0, (PEERS - 1) * ROWS)], sem)


def slot_rows(code):
    r = iota((PEERS * ROWS, 1), 0)
    t = r % ROWS
    wanted = jnp.where(t < 3 * CAP, (r // ROWS) * CAP + t % CAP, -2)
    return wanted == code


def halves(block, t):
    zero = jnp.zeros_like(block)
    left = jnp.where(t < CAP, block, zero)
    right = jnp.where((t >= CAP) & (t < 2 * CAP), block, zero)
    return jnp.concatenate([left, right], axis=1)


def attention(q_ref, k_ref, v_ref, u_ref, group, att, gq, gk, gv, after):
    one = jnp.where(group > 0, 1.0, 0.0)
    pad = jnp.zeros((HDIM - 2, N), F)
    q_bias = jnp.concatenate([-MASKED * (1 - one), -MASKED * one, pad], 0).astype(B)
    k_bias = jnp.concatenate([one, 1 - one, pad], 0).astype(B)
    ones = jnp.concatenate([jnp.ones((1, N), F), jnp.zeros((HDIM - 1, N), F)], 0).astype(B)
    scale = HDIM ** (-0.5)

    def head(h, carry):
        rows = pl.ds(pl.multiple_of(h * HDIM, HDIM), HDIM)
        q, k, v, u = q_ref[rows, :], k_ref[rows, :], v_ref[rows, :], u_ref[rows, :]
        qx = jnp.concatenate([q * B(scale), q_bias], 0)
        kx = jnp.concatenate([k, k_bias], 0)
        vx = jnp.concatenate([v, ones], 0)
        scores = dg(kx, qx, 0, 0)
        expo = jnp.exp(scores - jnp.max(scores, axis=0, keepdims=True))
        low = expo.astype(B)
        total = jnp.dot(vx, low, preferred_element_type=F)
        recip = 1.0 / total[HDIM : HDIM + 1]
        attended = total[:HDIM] * recip
        wide = u.astype(F)
        delta = jnp.sum(wide * attended, axis=0, keepdims=True)
        grad_probs = dg(v, u, 0, 0)
        grad_scores = (expo * ((grad_probs - delta) * (recip * scale))).astype(B)
        att[rows, :] = attended.astype(B)
        gq[rows, :] = jnp.dot(k, grad_scores, preferred_element_type=F).astype(B)
        gk[rows, :] = dg(q, grad_scores, 1, 1).astype(B)
        gv[rows, :] = dg((wide * recip).astype(B), low, 1, 1).astype(B)
        after(h)
        return carry

    lax.fori_loop(0, HEADS, head, 0)


def layer_kernel(
    rank_ref, feats_ref, patch_ref, gain_ref, w_qkv_ref, w_out_ref, d_mixed_ref,
    code_ref, mixed_ref, local_ref, ret_ref, sums_ref,
    send, got, hil, qkv, up, normed, low, low_rows, att, gqkv, chunk,
    half_send, half_got, piece_send, piece_got, done,
    go_sems, back_sems, half_sems, piece_sems, done_sems, last_sems,
):
    greet()
    me = lax.axis_index("seq")
    core = lax.rem(me, 2)
    chip = me // 2
    partner = chip * 2 + 1 - core
    own = pl.ds(pl.multiple_of(chip * PIECE, PIECE), PIECE)
    others = pl.ds(0, (CHIPS - 1) * PIECE)

    rank = rank_ref[...]
    owner = rank // N
    onehot = (iota((PEERS, N), 0) == owner).astype(F)
    upto = (iota((N, N), 0) <= iota((N, N), 1)).astype(F).astype(B)
    count = jnp.dot(onehot.astype(B), upto, preferred_element_type=F)
    slot = jnp.sum(count * onehot, axis=0, keepdims=True).astype(I) - 1
    code = jnp.where(owner == me, -1, owner * CAP + slot)
    code_ref[...] = code
    chosen = slot_rows(code).astype(F).astype(B)
    spot = rank % N
    k = iota((128, N), 0)
    extra = jnp.where(k == 0, spot // 32, jnp.where(k == 1, spot % 32, jnp.where(k == 2, 1, 0)))
    rows = jnp.dot(chosen, feats_ref[...], preferred_element_type=F)
    spots = dg(chosen, extra.astype(F).astype(B), 1, 1)
    t = iota((PEERS * ROWS, 128), 0) % ROWS
    block = jnp.where(t < CAP, rows[:, :128], jnp.where(t < 2 * CAP, rows[:, 128:], spots))
    send[...] = block.astype(B)
    mine = pl.ds(pl.multiple_of(me * ROWS, ROWS), ROWS)
    got[mine, :] = jnp.zeros((ROWS, 128), B)
    ret_ref[mine, :] = jnp.zeros((ROWS, 128), B)
    met()
    exchange(send, got, go_sems.at[0], go_sems.at[1])

    here = jnp.where(owner == me, spot, -1)
    p = iota((N, 1), 0)
    stay = (p == here).astype(F).astype(B)
    hil[...] = jnp.dot(stay, feats_ref[...], preferred_element_type=F).astype(B)
    up[...] = dg(w_out_ref[...], d_mixed_ref[...], 1, 1).astype(B)
    gain = jnp.broadcast_to(gain_ref[...], (8, C)).T[:, :1]
    await_exchange(got, go_sems.at[1])
    await_exchange(send, go_sems.at[0])

    arrived = got[...]
    weight = iota((16, 128), 1)
    weight = jnp.where(weight == 0, 32.0, jnp.where(weight < 2, 1.0, 0.0)).astype(B)
    valid = jnp.where(iota((16, 128), 1) == 2, 1.0, 0.0).astype(B)
    lane = iota((1, N), 1) % ROWS
    at = dg(weight, arrived, 1, 1)[:1]
    real = dg(valid, arrived, 1, 1)[:1]
    at = jnp.where(real > 0.5, at, -1.0)
    at = jnp.where(lane < 2 * CAP, -1.0, jnp.where(lane < 3 * CAP, at, -1.0))
    at = jnp.broadcast_to(at, (8, N))
    left = pltpu.roll(at, N - 2 * CAP, 1)[:1]
    right = pltpu.roll(at, N - CAP, 1)[:1]
    at = jnp.where(lane < CAP, left, jnp.where(lane < 2 * CAP, right, -1.0)).astype(I)
    come = (p == at).astype(F).astype(B)
    rows = hil[...].astype(F) + jnp.dot(come, halves(arrived, t), preferred_element_type=F)
    hil[...] = rows.astype(B)

    wide = rows.T
    centred = wide - jnp.mean(wide, axis=0, keepdims=True)
    recip = lax.rsqrt(jnp.mean(centred * centred, axis=0, keepdims=True) + EPS)
    normed[...] = centred * recip
    scaled = normed[...] * gain
    low[...] = scaled.astype(B)
    low_rows[...] = scaled.T.astype(B)
    qkv[...] = dg(w_qkv_ref[...], low[...], 0, 0).astype(B)

    def start_sum(g):
        span = slice(g * WIDE, (g + 1) * WIDE)
        parts = [gqkv[m * C + g * WIDE : m * C + (g + 1) * WIDE, :] for m in range(3)]
        sums = [jnp.dot(part, low_rows[...], preferred_element_type=F) for part in parts]
        sums.append(jnp.dot(att[span, :], d_mixed_ref[...], preferred_element_type=F))
        for m in range(4):
            for side in range(2):
                first = (m // 2) * HALF + side * 2 * WIDE + (m % 2) * WIDE
                chunk[first : first + WIDE, :] = sums[m][:, side * 128 : (side + 1) * 128]
        theirs = pl.ds(pl.multiple_of((1 - core) * HALF, HALF), HALF)
        half_send[g] = chunk[theirs, :].astype(B)
        remote(
            half_send.at[g], half_got.at[g], half_sems.at[g, 0], half_sems.at[g, 1], partner
        ).start()

    def scatter_sum(g):
        await_bytes(half_got.at[g], half_sems.at[g, 1])
        kept = chunk[pl.ds(pl.multiple_of(core * HALF, HALF), HALF), :]
        piece_send[g] = (kept + half_got[g].astype(F)).astype(B)
        piece_got[g, own, :] = piece_send[g, own, :]

        def scatter(step, carry):
            to = lax.rem(chip + step, CHIPS)
            theirs = pl.ds(pl.multiple_of(to * PIECE, PIECE), PIECE)
            remote(
                piece_send.at[g, theirs], piece_got.at[g, own],
                piece_sems.at[g, 0], piece_sems.at[g, 1], to * 2 + core,
            ).start()
            return carry

        lax.fori_loop(1, CHIPS, scatter, 0)

    def gather_sum(g):
        await_bytes(piece_got.at[g, others], piece_sems.at[g, 1])
        total = piece_got[g, 0:PIECE, :].astype(F)
        for j in range(1, CHIPS):
            total += piece_got[g, j * PIECE : (j + 1) * PIECE, :].astype(F)
        done[g, own, :] = total.astype(B)

        def gather(step, carry):
            to = lax.rem(chip + step, CHIPS)
            remote(
                done.at[g, own], done.at[g, own],
                done_sems.at[g, 0], done_sems.at[g, 1], to * 2 + core,
            ).start()
            return carry

        lax.fori_loop(1, CHIPS, gather, 0)

    def kept_half(g):
        return pl.ds(pl.multiple_of(g * 2 * HALF + core * HALF, HALF), HALF)

    def share_sum(g):
        await_bytes(done.at[g, others], done_sems.at[g, 1])
        remote(
            done.at[g], sums_ref.at[kept_half(g)], last_sems.at[g, 0], last_sems.at[g, 1], partner
        ).start()
        sums_ref[kept_half(g), :] = done[g]

    def end_sum(g):
        await_bytes(done.at[g], last_sems.at[g, 1])
        await_bytes(done.at[g], last_sems.at[g, 0])
        await_bytes(half_send.at[g], half_sems.at[g, 0])
        await_bytes(piece_send.at[g, others], piece_sems.at[g, 0])
        await_bytes(done.at[g, others], done_sems.at[g, 0])

    def after(h):
        per = HEADS // GROUPS
        for k, stage in enumerate((start_sum, scatter_sum, gather_sum, share_sum)):
            pl.when(h == per - 1 + 2 * k)(functools.partial(stage, 0))

    patch = patch_ref[...]
    attention(
        qkv.at[:C], qkv.at[C : 2 * C], qkv.at[2 * C :], up,
        (patch == patch[:, :1]).astype(F),
        att, gqkv.at[:C], gqkv.at[C : 2 * C], gqkv.at[2 * C :], after,
    )
    start_sum(1)

    grad_normed = jnp.dot(w_qkv_ref[...], gqkv[...], preferred_element_type=F)
    scaled = grad_normed * gain
    d_norm = recip * (
        scaled
        - jnp.mean(scaled, axis=0, keepdims=True)
        - normed[...] * jnp.mean(scaled * normed[...], axis=0, keepdims=True)
    )
    d_rows = (d_mixed_ref[...].astype(F).T + d_norm).astype(B)
    come = (p == at).astype(F).astype(B)
    back = jnp.dot(d_rows, come, preferred_element_type=F)
    back = jnp.where(lane < CAP, back[:128], jnp.where(lane < 2 * CAP, back[128:], 0.0))
    send[...] = back.T.astype(B)
    exchange(send, ret_ref, back_sems.at[0], back_sems.at[1])
    scatter_sum(1)
    stay = (p == here).astype(F).astype(B)
    local_ref[...] = jnp.dot(d_rows, stay, preferred_element_type=F).astype(B)
    mixed_ref[...] = (hil[...].astype(F) + dg(att[...], w_out_ref[...], 0, 0)).astype(B)
    gather_sum(1)
    await_exchange(ret_ref, back_sems.at[1])
    await_exchange(send, back_sems.at[0])
    share_sum(1)
    end_sum(0)
    end_sum(1)


def finish_kernel(
    code_ref, ret_ref, local_ref, sums_ref, w_qkv_ref, gain_ref,
    d_feats_ref, g_qkv_ref, g_out_ref, g_gain_ref,
):
    t = iota((PEERS * ROWS, 128), 0) % ROWS
    chosen = slot_rows(code_ref[...]).astype(F).astype(B)
    d_feats = dg(halves(ret_ref[...], t), chosen, 0, 0) + local_ref[...].astype(F)
    d_feats_ref[...] = d_feats.T.astype(B)
    for side in range(2):
        lanes = slice(side * 128, (side + 1) * 128)
        column = jnp.zeros((128, 128), F)
        for g in range(GROUPS):
            for m in range(4):
                first = (2 * g + m // 2) * HALF + side * 2 * WIDE + (m % 2) * WIDE
                part = sums_ref[first : first + WIDE, :].astype(F)
                if m < 3:
                    at = slice(m * C + g * WIDE, m * C + (g + 1) * WIDE)
                    part = part.T
                    g_qkv_ref[lanes, at] = part
                    column += part * w_qkv_ref[lanes, at].astype(F)
                else:
                    g_out_ref[g * WIDE : (g + 1) * WIDE, lanes] = part
        total_row = jnp.sum(column.T, axis=0, keepdims=True)
        g_gain_ref[:, lanes] = total_row / gain_ref[:, lanes]


def call(kernel, out_shapes, n_in, scratch=(), collective_id=None):
    params = dict(vmem_limit_bytes=VMEM)
    if collective_id is not None:
        params.update(collective_id=collective_id, has_side_effects=True)
    return pl.pallas_call(
        kernel,
        out_shape=[jax.ShapeDtypeStruct(s, d) for s, d in out_shapes],
        in_specs=[ANYWHERE] * n_in,
        out_specs=[ANYWHERE] * len(out_shapes),
        scratch_shapes=list(scratch),
        compiler_params=pltpu.CompilerParams(**params),
    )


def on_device(feats, hilbert_rank, patch_id, gain, w_qkv, w_out, d_mixed):
    rank = hilbert_rank.reshape(1, N)
    patch = patch_id.reshape(1, N)
    gain = gain.reshape(1, C)
    blocks = (PEERS * ROWS, 128)
    sums_shape = (GROUPS * 2 * HALF, 128)
    dma = pltpu.SemaphoreType.DMA
    by_point, by_channel = (N, C), (C, N)
    code, mixed, local, ret, sums = call(
        layer_kernel,
        [((1, N), I), (by_point, B), (by_channel, B), (blocks, B), (sums_shape, B)],
        7,
        [
            pltpu.VMEM(blocks, B), pltpu.VMEM(blocks, B), pltpu.VMEM(by_point, B),
            pltpu.VMEM((3 * C, N), B), pltpu.VMEM(by_channel, B), pltpu.VMEM(by_channel, F),
            pltpu.VMEM(by_channel, B), pltpu.VMEM(by_point, B), pltpu.VMEM(by_channel, B),
            pltpu.VMEM((3 * C, N), B), pltpu.VMEM((2 * HALF, 128), F),
        ]
        + [pltpu.VMEM((GROUPS, HALF, 128), B)] * 5
        + [dma((2,))] * 2
        + [dma((GROUPS, 2))] * 4,
        collective_id=0,
    )(rank, feats, patch, gain, w_qkv, w_out, d_mixed)
    d_feats, g_qkv, g_out, g_gain = call(
        finish_kernel, [((N, C), B), ((C, 3 * C), F), ((C, C), F), ((1, C), F)], 6
    )(code, ret, local, sums, w_qkv, gain)
    return (mixed, d_feats, g_qkv, g_out, g_gain.reshape(C))


def solution(mesh):
    return jax.shard_map(
        on_device,
        mesh=mesh,
        in_specs=(
            P(("rep", "seq"), None),
            P(("rep", "seq")),
            P(("rep", "seq")),
            P(),
            P(),
            P(),
            P(("rep", "seq"), None),
        ),
        out_specs=(
            P(("rep", "seq"), None),
            P(("rep", "seq"), None),
            P("rep", None),
            P("rep", None),
            P("rep"),
        ),
        check_vma=False,
    )
```

time: 123 us -> 110 us (0.89)
  Pallas kernels: 122 us -> 108 us
    pallas_call x3 -> x1, Pallas kernels: 118 us -> 105 us  [on_device(): call(layer_kernel, [((1, N), I), (by_point, B), (by_channel, B), (blocks,...]
where the time goes in v2:
time: 110 us
  Pallas kernels  108 us (98%)
    pallas_call x1, Pallas kernels, on_device(): call(layer_kernel, [((1, N), I), (by_point, B), (by_channel, B), (blocks,...  105 us
    pallas_call x1, Pallas kernels, on_device(): call(finish_kernel, [((N, C), B), ((C, 3 * C), F), ((C, C), F), ((1, C),...  3.46 us

profile of v2, /device:TPU:1, one launch (start us, length us, event | category | flops | bytes accessed | tf_op | source)
XLA Modules:
  0.0 109.6 jit_solution(16925283409914663635)
XLA Ops:
  0.6 104.7 %shard_map.110 = (s32[1,1024]{1,0:T(1,128)}, bf16[1024,256]{1,0:T(8,128)(2,1)}, bf16[256,1024]{1,0:T(8,128)(2,1)}, bf16[1024,128]{1,0:T(8,128)(2,1)}, bf16[2048,128]{1,0:T(8,128)(2,1)}) custom-call(s32[1,1024]{1,0:T(1,128)} %bitcast.4, bf16[1024,256]{1,0:T(8,128)(2,1)} %feats_ref.1, s32[1,1024]{1,0:T(1,128)} %bitcast.5, f32[1,256]{1,0:T(1,128)} %bitcast.6, ...), custom_call_target="tpu_custom_call" | custom-call | tf_op jit(solution)/shard_map/pallas_call | solution.py:364
  105.3 0.0 copy-start
  105.3 3.5 %shard_map.111 = (bf16[1024,256]{1,0:T(8,128)(2,1)}, f32[256,768]{1,0:T(8,128)}, f32[256,256]{1,0:T(8,128)}, f32[1,256]{1,0:T(1,128)}) custom-call(s32[1,1024]{1,0:T(1,128)} %get-tuple-element.15.code_ref, bf16[1024,128]{1,0:T(8,128)(2,1)} %get-tuple-element.16.ret_ref, bf16[256,1024]{1,0:T(8,128)(2,1)} %get-tuple-element.17.local_ref, ...), custom_call_target="tpu_custom_call" | custom-call | tf_op jit(solution)/shard_map/pallas_call | solution.py:379
  108.8 0.0 copy-done
  108.8 0.8 copy.13
Async XLA Ops:
  105.3 3.5 %copy-start = (bf16[1024,256]{1,0:T(8,128)(2,1)S(1)}, bf16[1024,256]{1,0:T(8,128)(2,1)}, u32[]{:S(2)}) copy-start(bf16[1024,256]{1,0:T(8,128)(2,1)} %get-tuple-element.28) | copy-start | bytes 1572868

commit v3 on v2

--- a/solution.py
+++ b/solution.py
@@ -25,6 +25,8 @@
 HALF = CHIPS * PIECE
 EPS = 1e-05
 MASKED = 1e30
+LOG2E = 1.4426950408889634
+UNROLL = 2
 VMEM = 56 << 20
 
 ANYWHERE = pl.BlockSpec(memory_space=pltpu.VMEM)
@@ -102,6 +104,11 @@
     return jnp.concatenate([left, right], axis=1)
 
 
+def split(x):
+    high = x.astype(B)
+    return high, (x - high.astype(F)).astype(B)
+
+
 def attention(q_ref, k_ref, v_ref, u_ref, group, att, gq, gk, gv, after):
     one = jnp.where(group > 0, 1.0, 0.0)
     pad = jnp.zeros((HDIM - 2, N), F)
@@ -110,30 +117,46 @@
     ones = jnp.concatenate([jnp.ones((1, N), F), jnp.zeros((HDIM - 1, N), F)], 0).astype(B)
     scale = HDIM ** (-0.5)
 
-    def head(h, carry):
+    def head(h):
         rows = pl.ds(pl.multiple_of(h * HDIM, HDIM), HDIM)
-        q, k, v, u = q_ref[rows, :], k_ref[rows, :], v_ref[rows, :], u_ref[rows, :]
-        qx = jnp.concatenate([q * B(scale), q_bias], 0)
-        kx = jnp.concatenate([k, k_bias], 0)
-        vx = jnp.concatenate([v, ones], 0)
-        scores = dg(kx, qx, 0, 0)
-        expo = jnp.exp(scores - jnp.max(scores, axis=0, keepdims=True))
-        low = expo.astype(B)
-        total = jnp.dot(vx, low, preferred_element_type=F)
-        recip = 1.0 / total[HDIM : HDIM + 1]
-        attended = total[:HDIM] * recip
-        wide = u.astype(F)
-        delta = jnp.sum(wide * attended, axis=0, keepdims=True)
-        grad_probs = dg(v, u, 0, 0)
-        grad_scores = (expo * ((grad_probs - delta) * (recip * scale))).astype(B)
+        q, k, v = q_ref[rows, :], k_ref[rows, :], v_ref[rows, :]
+        q_wide, k_wide, v_wide = q.astype(F), k.astype(F), v.astype(F)
+        u = u_ref[rows, :].astype(F)
+        center = jnp.mean(v_wide, axis=1, keepdims=True)
+        v_wide = v_wide - center
+        q_high, q_low = split(q_wide * (scale * LOG2E))
+        scores = dg(
+            jnp.concatenate([k, k, k_bias], 0), jnp.concatenate([q_high, q_low, q_bias], 0), 0, 0
+        )
+        low = jnp.exp2(scores - jnp.max(scores, axis=0, keepdims=True)).astype(B)
+        left = [v, ones, k] + [(v_wide[a : a + 1] * k_wide).astype(B) for a in range(HDIM)]
+        sums = jnp.dot(jnp.concatenate(left, 0), low, preferred_element_type=F)
+        recip = 1.0 / sums[HDIM : HDIM + 1]
+        attended = sums[:HDIM] * recip
+        delta = jnp.sum(u * (attended - center), axis=0, keepdims=True)
+        grad = -delta * sums[2 * HDIM : 3 * HDIM]
+        for a in range(HDIM):
+            grad += u[a : a + 1] * sums[(3 + a) * HDIM : (4 + a) * HDIM]
         att[rows, :] = attended.astype(B)
-        gq[rows, :] = jnp.dot(k, grad_scores, preferred_element_type=F).astype(B)
-        gk[rows, :] = dg(q, grad_scores, 1, 1).astype(B)
-        gv[rows, :] = dg((wide * recip).astype(B), low, 1, 1).astype(B)
-        after(h)
+        gq[rows, :] = (grad * (recip * scale)).astype(B)
+        u = u * recip
+        q_wide = q_wide * scale
+        left = [u.astype(B), (q_wide * (-delta * recip)).astype(B)]
+        left += [(u[a : a + 1] * q_wide).astype(B) for a in range(HDIM)]
+        sums = dg(jnp.concatenate(left, 0), low, 1, 1)
+        grad = sums[HDIM : 2 * HDIM]
+        for a in range(HDIM):
+            grad += v_wide[a : a + 1] * sums[(2 + a) * HDIM : (3 + a) * HDIM]
+        gv[rows, :] = sums[:HDIM].astype(B)
+        gk[rows, :] = grad.astype(B)
+
+    def heads(i, carry):
+        for j in range(UNROLL):
+            head(i * UNROLL + j)
+        after(i * UNROLL + UNROLL - 1)
         return carry
 
-    lax.fori_loop(0, HEADS, head, 0)
+    lax.fori_loop(0, HEADS // UNROLL, heads, 0)
 
 
 def layer_kernel(

time: 110 us -> 94 us (0.85)
  Pallas kernels: 108 us -> 92.4 us
    pallas_call x1, Pallas kernels: 105 us -> 88.9 us  [on_device(): call(layer_kernel, [((1, N), I), (by_point, B), (by_channel, B), (blocks,...]
where the time goes in v3:
time: 94 us; the launch traced here: 93.8 us
  Pallas kernels  92.4 us (98%)
    pallas_call x1, Pallas kernels, on_device(): call(layer_kernel, [((1, N), I), (by_point, B), (by_channel, B), (blocks,...  88.9 us
    pallas_call x1, Pallas kernels, on_device(): call(finish_kernel, [((N, C), B), ((C, 3 * C), F), ((C, C), F), ((1, C),...  3.46 us

profile of v3, /device:TPU:1, one launch (start us, length us, event | category | flops | bytes accessed | tf_op | source)
XLA Modules:
  0.0 93.8 jit_solution(4275083458344723993)
XLA Ops:
  0.6 88.9 %shard_map.110 = (s32[1,1024]{1,0:T(1,128)}, bf16[1024,256]{1,0:T(8,128)(2,1)}, bf16[256,1024]{1,0:T(8,128)(2,1)}, bf16[1024,128]{1,0:T(8,128)(2,1)}, bf16[2048,128]{1,0:T(8,128)(2,1)}) custom-call(s32[1,1024]{1,0:T(1,128)} %bitcast.4, bf16[1024,256]{1,0:T(8,128)(2,1)} %feats_ref.1, s32[1,1024]{1,0:T(1,128)} %bitcast.5, f32[1,256]{1,0:T(1,128)} %bitcast.6, ...), custom_call_target="tpu_custom_call" | custom-call | tf_op jit(solution)/shard_map/pallas_call | solution.py:387
  89.6 0.0 copy-start
  89.6 3.5 %shard_map.111 = (bf16[1024,256]{1,0:T(8,128)(2,1)}, f32[256,768]{1,0:T(8,128)}, f32[256,256]{1,0:T(8,128)}, f32[1,256]{1,0:T(1,128)}) custom-call(s32[1,1024]{1,0:T(1,128)} %get-tuple-element.15.code_ref, bf16[1024,128]{1,0:T(8,128)(2,1)} %get-tuple-element.16.ret_ref, bf16[256,1024]{1,0:T(8,128)(2,1)} %get-tuple-element.17.local_ref, ...), custom_call_target="tpu_custom_call" | custom-call | tf_op jit(solution)/shard_map/pallas_call | solution.py:402
  93.1 0.0 copy-done
  93.1 0.8 copy.13
Async XLA Ops:
  89.6 3.5 %copy-start = (bf16[1024,256]{1,0:T(8,128)(2,1)S(1)}, bf16[1024,256]{1,0:T(8,128)(2,1)}, u32[]{:S(2)}) copy-start(bf16[1024,256]{1,0:T(8,128)(2,1)} %get-tuple-element.28) | copy-start | bytes 1572868

commit v4 on v3

--- a/solution.py
+++ b/solution.py
@@ -17,12 +17,14 @@
 HEADS = C // HDIM
 PEERS = 64
 CAP = 4
-ROWS = 16
+SLOTS = PEERS * CAP
 CHIPS = 32
-GROUPS = 2
-WIDE = C // GROUPS
+WIDE = C // 2
 PIECE = 16
 HALF = CHIPS * PIECE
+PAIR = 2 * HDIM
+OWNERS = 16
+PAIRS = 4
 EPS = 1e-05
 MASKED = 1e30
 LOG2E = 1.4426950408889634
@@ -75,33 +77,21 @@
 
 def exchange(src, dst, send_sem, recv_sem):
     me = lax.axis_index("seq")
-    mine = pl.ds(pl.multiple_of(me * ROWS, ROWS), ROWS)
 
     def send(step, carry):
         peer = lax.rem(me + step, PEERS)
-        theirs = pl.ds(pl.multiple_of(peer * ROWS, ROWS), ROWS)
-        remote(src.at[theirs], dst.at[mine], send_sem, recv_sem, peer).start()
+        remote(src.at[peer], dst.at[me], send_sem, recv_sem, peer).start()
         return carry
 
     lax.fori_loop(1, PEERS, send, 0)
 
 
 def await_exchange(ref, sem):
-    await_bytes(ref.at[pl.ds(0, (PEERS - 1) * ROWS)], sem)
+    await_bytes(ref.at[pl.ds(0, PEERS - 1)], sem)
 
 
 def slot_rows(code):
-    r = iota((PEERS * ROWS, 1), 0)
-    t = r % ROWS
-    wanted = jnp.where(t < 3 * CAP, (r // ROWS) * CAP + t % CAP, -2)
-    return wanted == code
-
-
-def halves(block, t):
-    zero = jnp.zeros_like(block)
-    left = jnp.where(t < CAP, block, zero)
-    right = jnp.where((t >= CAP) & (t < 2 * CAP), block, zero)
-    return jnp.concatenate([left, right], axis=1)
+    return (iota((SLOTS, 1), 0) == code).astype(F).astype(B)
 
 
 def split(x):
@@ -161,10 +151,11 @@
 
 def layer_kernel(
     rank_ref, feats_ref, patch_ref, gain_ref, w_qkv_ref, w_out_ref, d_mixed_ref,
-    code_ref, mixed_ref, local_ref, ret_ref, sums_ref,
-    send, got, hil, qkv, up, normed, low, low_rows, att, gqkv, chunk,
-    half_send, half_got, piece_send, piece_got, done,
-    go_sems, back_sems, half_sems, piece_sems, done_sems, last_sems,
+    code_ref, mixed_ref, local_ref, ret_ref, sums_ref, tails_ref,
+    send, got, flat, back_send, back_got,
+    hil, qkv, up, normed, low, low_rows, att, gqkv, chunk,
+    half_send, half_got, piece_send, piece_got, done, pair_send, pair_got,
+    go_sems, back_sems, half_sems, piece_sems, done_sems, last_sems, pair_sems, tail_sems,
 ):
     greet()
     me = lax.axis_index("seq")
@@ -172,7 +163,9 @@
     chip = me // 2
     partner = chip * 2 + 1 - core
     own = pl.ds(pl.multiple_of(chip * PIECE, PIECE), PIECE)
+    mine = pl.ds(pl.multiple_of(me * PIECE, PIECE), PIECE)
     others = pl.ds(0, (CHIPS - 1) * PIECE)
+    peers = pl.ds(0, (PEERS - 1) * PIECE)
 
     rank = rank_ref[...]
     owner = rank // N
@@ -182,18 +175,17 @@
     slot = jnp.sum(count * onehot, axis=0, keepdims=True).astype(I) - 1
     code = jnp.where(owner == me, -1, owner * CAP + slot)
     code_ref[...] = code
-    chosen = slot_rows(code).astype(F).astype(B)
+    chosen = slot_rows(code)
     spot = rank % N
     k = iota((128, N), 0)
     extra = jnp.where(k == 0, spot // 32, jnp.where(k == 1, spot % 32, jnp.where(k == 2, 1, 0)))
     rows = jnp.dot(chosen, feats_ref[...], preferred_element_type=F)
     spots = dg(chosen, extra.astype(F).astype(B), 1, 1)
-    t = iota((PEERS * ROWS, 128), 0) % ROWS
-    block = jnp.where(t < CAP, rows[:, :128], jnp.where(t < 2 * CAP, rows[:, 128:], spots))
-    send[...] = block.astype(B)
-    mine = pl.ds(pl.multiple_of(me * ROWS, ROWS), ROWS)
-    got[mine, :] = jnp.zeros((ROWS, 128), B)
-    ret_ref[mine, :] = jnp.zeros((ROWS, 128), B)
+    for o in range(PEERS):
+        send[o, :, :C] = rows[o * CAP : (o + 1) * CAP].astype(B)
+        send[o, :, C:] = spots[o * CAP : (o + 1) * CAP].astype(B)
+    got[me] = jnp.zeros((CAP, C + 128), B)
+    back_got[me] = jnp.zeros((CAP, C), B)
     met()
     exchange(send, got, go_sems.at[0], go_sems.at[1])
 
@@ -206,21 +198,17 @@
     await_exchange(got, go_sems.at[1])
     await_exchange(send, go_sems.at[0])
 
-    arrived = got[...]
+    for o in range(PEERS):
+        flat[o * CAP : (o + 1) * CAP, :] = got[o].astype(F)
+    spots = flat[:, C:].astype(B)
     weight = iota((16, 128), 1)
     weight = jnp.where(weight == 0, 32.0, jnp.where(weight < 2, 1.0, 0.0)).astype(B)
     valid = jnp.where(iota((16, 128), 1) == 2, 1.0, 0.0).astype(B)
-    lane = iota((1, N), 1) % ROWS
-    at = dg(weight, arrived, 1, 1)[:1]
-    real = dg(valid, arrived, 1, 1)[:1]
-    at = jnp.where(real > 0.5, at, -1.0)
-    at = jnp.where(lane < 2 * CAP, -1.0, jnp.where(lane < 3 * CAP, at, -1.0))
-    at = jnp.broadcast_to(at, (8, N))
-    left = pltpu.roll(at, N - 2 * CAP, 1)[:1]
-    right = pltpu.roll(at, N - CAP, 1)[:1]
-    at = jnp.where(lane < CAP, left, jnp.where(lane < 2 * CAP, right, -1.0)).astype(I)
+    at = dg(weight, spots, 1, 1)[:1]
+    at = jnp.where(dg(valid, spots, 1, 1)[:1] > 0.5, at, -1.0).astype(I)
     come = (p == at).astype(F).astype(B)
-    rows = hil[...].astype(F) + jnp.dot(come, halves(arrived, t), preferred_element_type=F)
+    rows = hil[...].astype(F)
+    rows += jnp.dot(come, flat[:, :C].astype(B), preferred_element_type=F)
     hil[...] = rows.astype(B)
 
     wide = rows.T
@@ -232,76 +220,122 @@
     low_rows[...] = scaled.T.astype(B)
     qkv[...] = dg(w_qkv_ref[...], low[...], 0, 0).astype(B)
 
-    def start_sum(g):
-        span = slice(g * WIDE, (g + 1) * WIDE)
-        parts = [gqkv[m * C + g * WIDE : m * C + (g + 1) * WIDE, :] for m in range(3)]
+    def gradients(first, wide):
+        parts = [gqkv[pl.ds(m * C + first, wide), :] for m in range(3)]
         sums = [jnp.dot(part, low_rows[...], preferred_element_type=F) for part in parts]
-        sums.append(jnp.dot(att[span, :], d_mixed_ref[...], preferred_element_type=F))
+        span = pl.ds(first, wide)
+        return sums + [jnp.dot(att[span, :], d_mixed_ref[...], preferred_element_type=F)]
+
+    def start_sum():
+        sums = gradients(0, WIDE)
         for m in range(4):
             for side in range(2):
                 first = (m // 2) * HALF + side * 2 * WIDE + (m % 2) * WIDE
                 chunk[first : first + WIDE, :] = sums[m][:, side * 128 : (side + 1) * 128]
         theirs = pl.ds(pl.multiple_of((1 - core) * HALF, HALF), HALF)
-        half_send[g] = chunk[theirs, :].astype(B)
-        remote(
-            half_send.at[g], half_got.at[g], half_sems.at[g, 0], half_sems.at[g, 1], partner
-        ).start()
-
-    def scatter_sum(g):
-        await_bytes(half_got.at[g], half_sems.at[g, 1])
+        half_send[...] = chunk[theirs, :].astype(B)
+        remote(half_send, half_got, half_sems.at[0], half_sems.at[1], partner).start()
+
+    def scatter_sum():
+        await_bytes(half_got, half_sems.at[1])
         kept = chunk[pl.ds(pl.multiple_of(core * HALF, HALF), HALF), :]
-        piece_send[g] = (kept + half_got[g].astype(F)).astype(B)
-        piece_got[g, own, :] = piece_send[g, own, :]
+        piece_send[...] = (kept + half_got[...].astype(F)).astype(B)
+        piece_got[own, :] = piece_send[own, :]
 
         def scatter(step, carry):
             to = lax.rem(chip + step, CHIPS)
             theirs = pl.ds(pl.multiple_of(to * PIECE, PIECE), PIECE)
             remote(
-                piece_send.at[g, theirs], piece_got.at[g, own],
-                piece_sems.at[g, 0], piece_sems.at[g, 1], to * 2 + core,
+                piece_send.at[theirs], piece_got.at[own],
+                piece_sems.at[0], piece_sems.at[1], to * 2 + core,
             ).start()
             return carry
 
         lax.fori_loop(1, CHIPS, scatter, 0)
 
-    def gather_sum(g):
-        await_bytes(piece_got.at[g, others], piece_sems.at[g, 1])
-        total = piece_got[g, 0:PIECE, :].astype(F)
-        for j in range(1, CHIPS):
-            total += piece_got[g, j * PIECE : (j + 1) * PIECE, :].astype(F)
-        done[g, own, :] = total.astype(B)
+    def total_of(pieces, count):
+        total = pieces[0:PIECE, :].astype(F)
+        for j in range(1, count):
+            total += pieces[j * PIECE : (j + 1) * PIECE, :].astype(F)
+        return total.astype(B)
+
+    def gather_sum():
+        await_bytes(piece_got.at[others], piece_sems.at[1])
+        done[own, :] = total_of(piece_got, CHIPS)
 
         def gather(step, carry):
             to = lax.rem(chip + step, CHIPS)
             remote(
-                done.at[g, own], done.at[g, own],
-                done_sems.at[g, 0], done_sems.at[g, 1], to * 2 + core,
+                done.at[own], done.at[own], done_sems.at[0], done_sems.at[1], to * 2 + core
             ).start()
             return carry
 
         lax.fori_loop(1, CHIPS, gather, 0)
 
-    def kept_half(g):
-        return pl.ds(pl.multiple_of(g * 2 * HALF + core * HALF, HALF), HALF)
-
-    def share_sum(g):
-        await_bytes(done.at[g, others], done_sems.at[g, 1])
-        remote(
-            done.at[g], sums_ref.at[kept_half(g)], last_sems.at[g, 0], last_sems.at[g, 1], partner
-        ).start()
-        sums_ref[kept_half(g), :] = done[g]
-
-    def end_sum(g):
-        await_bytes(done.at[g], last_sems.at[g, 1])
-        await_bytes(done.at[g], last_sems.at[g, 0])
-        await_bytes(half_send.at[g], half_sems.at[g, 0])
-        await_bytes(piece_send.at[g, others], piece_sems.at[g, 0])
-        await_bytes(done.at[g, others], done_sems.at[g, 0])
+    def share_sum():
+        await_bytes(done.at[others], done_sems.at[1])
+        kept = pl.ds(pl.multiple_of(core * HALF, HALF), HALF)
+        remote(done, sums_ref.at[kept], last_sems.at[0], last_sems.at[1], partner).start()
+        sums_ref[kept, :] = done[...]
+
+    def end_sum():
+        await_bytes(done, last_sems.at[1])
+        await_bytes(done, last_sems.at[0])
+        await_bytes(half_send, half_sems.at[0])
+        await_bytes(piece_send.at[others], piece_sems.at[0])
+        await_bytes(done.at[others], done_sems.at[0])
+
+    turn = lax.rem(me, PAIRS)
+
+    def start_pair(c):
+        sums = gradients(pl.multiple_of(WIDE + c * PAIR, PAIR), PAIR)
+        for m in range(4):
+            for side in range(2):
+                first = (side * 4 + m) * PAIR
+                pair_send[c, first : first + PAIR, :] = sums[m][
+                    :, side * 128 : (side + 1) * 128
+                ].astype(B)
+
+        def piece(m):
+            return pair_send.at[c, pl.ds(pl.multiple_of(m * PIECE, PIECE), PIECE)]
+
+        def scatter(step, carry):
+            m = lax.rem(me // PAIRS + step, OWNERS)
+            remote(
+                piece(m), pair_got.at[mine], pair_sems.at[0], pair_sems.at[1], m * PAIRS + c
+            ).start()
+            return carry
+
+        @pl.when(turn == c)
+        def _():
+            pair_got[mine, :] = piece(me // PAIRS)[...]
+
+        @pl.when(turn != c)
+        def _():
+            scatter(0, 0)
+
+        lax.fori_loop(1, OWNERS, scatter, 0)
+
+    def finish_pair():
+        await_bytes(pair_got.at[peers], pair_sems.at[1])
+        tails_ref[mine, :] = total_of(pair_got, PEERS)
+
+        def gather(step, carry):
+            peer = lax.rem(me + step, PEERS)
+            remote(
+                tails_ref.at[mine], tails_ref.at[mine], tail_sems.at[0], tail_sems.at[1], peer
+            ).start()
+            return carry
+
+        lax.fori_loop(1, PEERS, gather, 0)
 
     def after(h):
-        per = HEADS // GROUPS
         for k, stage in enumerate((start_sum, scatter_sum, gather_sum, share_sum)):
-            pl.when(h == per - 1 + 2 * k)(functools.partial(stage, 0))
+            pl.when(h == HEADS // 2 - 1 + 2 * k)(stage)
+        first = HEADS // 2 + 1
+        for c in range(2):
+            pl.when((h == first + 2 * c + 4) & (turn == c))(finish_pair)
+        pl.when(h >= first)(lambda: start_pair((h - first) // 2))
 
     patch = patch_ref[...]
     attention(
@@ -309,7 +343,6 @@
         (patch == patch[:, :1]).astype(F),
         att, gqkv.at[:C], gqkv.at[C : 2 * C], gqkv.at[2 * C :], after,
     )
-    start_sum(1)
 
     grad_normed = jnp.dot(w_qkv_ref[...], gqkv[...], preferred_element_type=F)
     scaled = grad_normed * gain
@@ -320,37 +353,46 @@
     )
     d_rows = (d_mixed_ref[...].astype(F).T + d_norm).astype(B)
     come = (p == at).astype(F).astype(B)
-    back = jnp.dot(d_rows, come, preferred_element_type=F)
-    back = jnp.where(lane < CAP, back[:128], jnp.where(lane < 2 * CAP, back[128:], 0.0))
-    send[...] = back.T.astype(B)
-    exchange(send, ret_ref, back_sems.at[0], back_sems.at[1])
-    scatter_sum(1)
+    back = jnp.dot(d_rows, come, preferred_element_type=F).T
+    for o in range(PEERS):
+        back_send[o] = back[o * CAP : (o + 1) * CAP].astype(B)
+    exchange(back_send, back_got, back_sems.at[0], back_sems.at[1])
+    pl.when(turn >= 2)(finish_pair)
     stay = (p == here).astype(F).astype(B)
     local_ref[...] = jnp.dot(d_rows, stay, preferred_element_type=F).astype(B)
     mixed_ref[...] = (hil[...].astype(F) + dg(att[...], w_out_ref[...], 0, 0)).astype(B)
-    gather_sum(1)
-    await_exchange(ret_ref, back_sems.at[1])
-    await_exchange(send, back_sems.at[0])
-    share_sum(1)
-    end_sum(0)
-    end_sum(1)
+    end_sum()
+    await_exchange(back_got, back_sems.at[1])
+    await_exchange(back_send, back_sems.at[0])
+    for o in range(PEERS):
+        ret_ref[o * CAP : (o + 1) * CAP, :] = back_got[o]
+    await_bytes(pair_got.at[peers], pair_sems.at[0])
+    await_bytes(tails_ref.at[peers], tail_sems.at[1])
+    await_bytes(tails_ref.at[peers], tail_sems.at[0])
 
 
 def finish_kernel(
-    code_ref, ret_ref, local_ref, sums_ref, w_qkv_ref, gain_ref,
+    code_ref, ret_ref, local_ref, sums_ref, tails_ref, w_qkv_ref, gain_ref,
     d_feats_ref, g_qkv_ref, g_out_ref, g_gain_ref,
 ):
-    t = iota((PEERS * ROWS, 128), 0) % ROWS
-    chosen = slot_rows(code_ref[...]).astype(F).astype(B)
-    d_feats = dg(halves(ret_ref[...], t), chosen, 0, 0) + local_ref[...].astype(F)
+    d_feats = dg(ret_ref[...], slot_rows(code_ref[...]), 0, 0) + local_ref[...].astype(F)
     d_feats_ref[...] = d_feats.T.astype(B)
+
+    def sums(m, side):
+        first = (m // 2) * HALF + side * 2 * WIDE + (m % 2) * WIDE
+        yield sums_ref[first : first + WIDE, :].astype(F)
+        tails = []
+        for c in range(PAIRS):
+            for part in range(2):
+                first = (((side * 4 + m) * 2 + part) * PAIRS + c) * PIECE
+                tails.append(tails_ref[first : first + PIECE, :].astype(F))
+        yield jnp.concatenate(tails, 0)
+
     for side in range(2):
         lanes = slice(side * 128, (side + 1) * 128)
         column = jnp.zeros((128, 128), F)
-        for g in range(GROUPS):
-            for m in range(4):
-                first = (2 * g + m // 2) * HALF + side * 2 * WIDE + (m % 2) * WIDE
-                part = sums_ref[first : first + WIDE, :].astype(F)
+        for m in range(4):
+            for g, part in enumerate(sums(m, side)):
                 if m < 3:
                     at = slice(m * C + g * WIDE, m * C + (g + 1) * WIDE)
                     part = part.T
@@ -380,28 +422,29 @@
     rank = hilbert_rank.reshape(1, N)
     patch = patch_id.reshape(1, N)
     gain = gain.reshape(1, C)
-    blocks = (PEERS * ROWS, 128)
-    sums_shape = (GROUPS * 2 * HALF, 128)
     dma = pltpu.SemaphoreType.DMA
     by_point, by_channel = (N, C), (C, N)
-    code, mixed, local, ret, sums = call(
+    half, whole = (HALF, 128), (2 * HALF, 128)
+    out_block, back_block = (PEERS, CAP, C + 128), (PEERS, CAP, C)
+    code, mixed, local, ret, sums, tails = call(
         layer_kernel,
-        [((1, N), I), (by_point, B), (by_channel, B), (blocks, B), (sums_shape, B)],
+        [((1, N), I), (by_point, B), (by_channel, B), ((SLOTS, C), B), (whole, B), (whole, B)],
         7,
         [
-            pltpu.VMEM(blocks, B), pltpu.VMEM(blocks, B), pltpu.VMEM(by_point, B),
+            pltpu.VMEM(out_block, B), pltpu.VMEM(out_block, B), pltpu.VMEM((SLOTS, C + 128), F),
+            pltpu.VMEM(back_block, B), pltpu.VMEM(back_block, B), pltpu.VMEM(by_point, B),
             pltpu.VMEM((3 * C, N), B), pltpu.VMEM(by_channel, B), pltpu.VMEM(by_channel, F),
             pltpu.VMEM(by_channel, B), pltpu.VMEM(by_point, B), pltpu.VMEM(by_channel, B),
-            pltpu.VMEM((3 * C, N), B), pltpu.VMEM((2 * HALF, 128), F),
+            pltpu.VMEM((3 * C, N), B), pltpu.VMEM(whole, F),
         ]
-        + [pltpu.VMEM((GROUPS, HALF, 128), B)] * 5
-        + [dma((2,))] * 2
-        + [dma((GROUPS, 2))] * 4,
+        + [pltpu.VMEM(half, B)] * 5
+        + [pltpu.VMEM((PAIRS, OWNERS * PIECE, 128), B), pltpu.VMEM(whole, B)]
+        + [dma((2,))] * 8,
         collective_id=0,
     )(rank, feats, patch, gain, w_qkv, w_out, d_mixed)
     d_feats, g_qkv, g_out, g_gain = call(
-        finish_kernel, [((N, C), B), ((C, 3 * C), F), ((C, C), F), ((1, C), F)], 6
-    )(code, ret, local, sums, w_qkv, gain)
+        finish_kernel, [((N, C), B), ((C, 3 * C), F), ((C, C), F), ((1, C), F)], 7
+    )(code, ret, local, sums, tails, w_qkv, gain)
     return (mixed, d_feats, g_qkv, g_out, g_gain.reshape(C))
 
 

time: 94 us -> 84.9 us (0.903)
  Pallas kernels: 92.4 us -> 83.3 us
    pallas_call x1, Pallas kernels: 88.9 us -> 80.3 us  [on_device(): call(layer_kernel, [((1, N), I), (by_point, B), (by_channel, B), ((SLOTS,...]
where the time goes in v4:
time: 84.9 us; the launch traced here: 84.7 us
  Pallas kernels  83.3 us (98%)
    pallas_call x1, Pallas kernels, on_device(): call(layer_kernel, [((1, N), I), (by_point, B), (by_channel, B), ((SLOTS,...  80.3 us
    pallas_call x1, Pallas kernels, on_device(): call(finish_kernel, [((N, C), B), ((C, 3 * C), F), ((C, C), F), ((1, C),...  3.03 us

profile of v4, /device:TPU:1, one launch (start us, length us, event | category | flops | bytes accessed | tf_op | source)
XLA Modules:
  0.0 84.7 jit_solution(16022270968648482909)
XLA Ops:
  0.6 80.3 %shard_map.110 = (s32[1,1024]{1,0:T(1,128)}, bf16[1024,256]{1,0:T(8,128)(2,1)}, bf16[256,1024]{1,0:T(8,128)(2,1)}, bf16[256,256]{1,0:T(8,128)(2,1)}, bf16[1024,1...) custom-call(s32[1,1024]{1,0:T(1,128)} %bitcast.4, bf16[1024,256]{1,0:T(8,128)(2,1)} %feats_ref.1, s32[1,1024]{1,0:T(1,128)} %bitcast.5, ...), custom_call_target="tpu_custom_call" | custom-call | tf_op jit(solution)/shard_map/pallas_call | solution.py:429
  80.9 0.0 copy-start
  80.9 3.0 %shard_map.111 = (bf16[1024,256]{1,0:T(8,128)(2,1)}, f32[256,768]{1,0:T(8,128)}, f32[256,256]{1,0:T(8,128)}, f32[1,256]{1,0:T(1,128)}) custom-call(s32[1,1024]{1,0:T(1,128)} %get-tuple-element.16.code_ref, bf16[256,256]{1,0:T(8,128)(2,1)} %get-tuple-element.17.ret_ref, bf16[256,1024]{1,0:T(8,128)(2,1)} %get-tuple-element.18.local_ref, ...), custom_call_target="tpu_custom_call" | custom-call | tf_op jit(solution)/shard_map/pallas_call | solution.py:445
  83.9 0.0 copy-done
  83.9 0.8 copy.13
Async XLA Ops:
  80.9 3.0 %copy-start = (bf16[1024,256]{1,0:T(8,128)(2,1)S(1)}, bf16[1024,256]{1,0:T(8,128)(2,1)}, u32[]{:S(2)}) copy-start(bf16[1024,256]{1,0:T(8,128)(2,1)} %get-tuple-element.30) | copy-start | bytes 1572868

commit v5 on v4

--- a/solution.py
+++ b/solution.py
@@ -28,10 +28,10 @@
 EPS = 1e-05
 MASKED = 1e30
 LOG2E = 1.4426950408889634
-UNROLL = 2
+HALVES = 2
 VMEM = 56 << 20
 
-ANYWHERE = pl.BlockSpec(memory_space=pltpu.VMEM)
+VECTOR = pl.BlockSpec(memory_space=pltpu.VMEM)
 
 
 def dg(a, b, ca, cb):
@@ -46,14 +46,14 @@
     me = lax.axis_index("seq")
     barrier = pltpu.get_barrier_semaphore()
 
-    def signal(step, carry):
+    def signal(step):
         peer = lax.rem(me + step, PEERS)
         pl.semaphore_signal(
             barrier, inc=1, device_id={"seq": peer}, device_id_type=pl.DeviceIdType.MESH
         )
-        return carry
-
-    lax.fori_loop(1, PEERS, signal, 0)
+
+    for step in range(1, PEERS):
+        signal(step)
 
 
 def met():
@@ -78,12 +78,12 @@
 def exchange(src, dst, send_sem, recv_sem):
     me = lax.axis_index("seq")
 
-    def send(step, carry):
+    def send(step):
         peer = lax.rem(me + step, PEERS)
         remote(src.at[peer], dst.at[me], send_sem, recv_sem, peer).start()
-        return carry
-
-    lax.fori_loop(1, PEERS, send, 0)
+
+    for step in range(1, PEERS):
+        send(step)
 
 
 def await_exchange(ref, sem):
@@ -99,7 +99,7 @@
     return high, (x - high.astype(F)).astype(B)
 
 
-def attention(q_ref, k_ref, v_ref, u_ref, group, att, gq, gk, gv, after):
+def attention(q_ref, k_ref, v_ref, u_ref, group, att, gq, gk, gv, expo, after):
     one = jnp.where(group > 0, 1.0, 0.0)
     pad = jnp.zeros((HDIM - 2, N), F)
     q_bias = jnp.concatenate([-MASKED * (1 - one), -MASKED * one, pad], 0).astype(B)
@@ -107,46 +107,77 @@
     ones = jnp.concatenate([jnp.ones((1, N), F), jnp.zeros((HDIM - 1, N), F)], 0).astype(B)
     scale = HDIM ** (-0.5)
 
-    def head(h):
-        rows = pl.ds(pl.multiple_of(h * HDIM, HDIM), HDIM)
-        q, k, v = q_ref[rows, :], k_ref[rows, :], v_ref[rows, :]
-        q_wide, k_wide, v_wide = q.astype(F), k.astype(F), v.astype(F)
-        u = u_ref[rows, :].astype(F)
+    def rows_of(h):
+        return pl.ds(pl.multiple_of(h * HDIM, HDIM), HDIM)
+
+    def softmax_of(h, slot):
+        rows = rows_of(h)
+        q_high, q_low = split(q_ref[rows, :].astype(F) * (scale * LOG2E))
+        query = jnp.concatenate([q_high, q_low, q_bias], 0)
+        k = k_ref[rows, :]
+        keys = jnp.concatenate([k, k, k_bias], 0).astype(F).T.astype(B)
+        wide = N // (2 * HALVES)
+
+        def block(b):
+            span = slice(b * wide, (b + 1) * wide)
+            scores = jnp.dot(keys, query[:, span], preferred_element_type=F)
+            top = jnp.max(scores, axis=0, keepdims=True)
+            expo[slot, :, span] = jnp.exp2(scores - top).astype(B)
+
+        return block
+
+    def head(h, slot, beside):
+        rows = rows_of(h)
+        k, v = k_ref[rows, :], v_ref[rows, :]
+        q_wide, k_wide, v_wide = q_ref[rows, :].astype(F) * scale, k.astype(F), v.astype(F)
+        u_wide = u_ref[rows, :].astype(F)
         center = jnp.mean(v_wide, axis=1, keepdims=True)
         v_wide = v_wide - center
-        q_high, q_low = split(q_wide * (scale * LOG2E))
-        scores = dg(
-            jnp.concatenate([k, k, k_bias], 0), jnp.concatenate([q_high, q_low, q_bias], 0), 0, 0
-        )
-        low = jnp.exp2(scores - jnp.max(scores, axis=0, keepdims=True)).astype(B)
         left = [v, ones, k] + [(v_wide[a : a + 1] * k_wide).astype(B) for a in range(HDIM)]
-        sums = jnp.dot(jnp.concatenate(left, 0), low, preferred_element_type=F)
-        recip = 1.0 / sums[HDIM : HDIM + 1]
-        attended = sums[:HDIM] * recip
-        delta = jnp.sum(u * (attended - center), axis=0, keepdims=True)
-        grad = -delta * sums[2 * HDIM : 3 * HDIM]
-        for a in range(HDIM):
-            grad += u[a : a + 1] * sums[(3 + a) * HDIM : (4 + a) * HDIM]
-        att[rows, :] = attended.astype(B)
-        gq[rows, :] = (grad * (recip * scale)).astype(B)
-        u = u * recip
-        q_wide = q_wide * scale
-        left = [u.astype(B), (q_wide * (-delta * recip)).astype(B)]
-        left += [(u[a : a + 1] * q_wide).astype(B) for a in range(HDIM)]
-        sums = dg(jnp.concatenate(left, 0), low, 1, 1)
-        grad = sums[HDIM : 2 * HDIM]
-        for a in range(HDIM):
-            grad += v_wide[a : a + 1] * sums[(2 + a) * HDIM : (3 + a) * HDIM]
-        gv[rows, :] = sums[:HDIM].astype(B)
-        gk[rows, :] = grad.astype(B)
+        left = jnp.concatenate(left, 0)
+        wide = N // HALVES
+        spans = [slice(b * wide, (b + 1) * wide) for b in range(HALVES)]
+        right = []
+        for b, span in enumerate(spans):
+            beside(b)
+            sums = jnp.dot(left, expo[slot, :, span], preferred_element_type=F)
+            recip = 1.0 / sums[HDIM : HDIM + 1]
+            attended = sums[:HDIM] * recip
+            u = u_wide[:, span]
+            delta = jnp.sum(u * (attended - center), axis=0, keepdims=True)
+            grad = -delta * sums[2 * HDIM : 3 * HDIM]
+            for a in range(HDIM):
+                grad += u[a : a + 1] * sums[(3 + a) * HDIM : (4 + a) * HDIM]
+            att[rows, span] = attended.astype(B)
+            gq[rows, span] = (grad * (recip * scale)).astype(B)
+            u = u * recip
+            q = q_wide[:, span]
+            parts = [u.astype(B), (q * (-delta * recip)).astype(B)]
+            parts += [(u[a : a + 1] * q).astype(B) for a in range(HDIM)]
+            right.append(jnp.concatenate(parts, 0))
+        right = jnp.concatenate(right, 1)
+        for b, span in enumerate(spans):
+            beside(HALVES + b)
+            sums = dg(right, expo[slot, span, :], 1, 1)
+            grad = sums[HDIM : 2 * HDIM]
+            for a in range(HDIM):
+                grad += v_wide[a : a + 1, span] * sums[(2 + a) * HDIM : (3 + a) * HDIM]
+            gv[rows, span] = sums[:HDIM].astype(B)
+            gk[rows, span] = grad.astype(B)
+
+    first = softmax_of(0, 0)
+    for b in range(2 * HALVES):
+        first(b)
 
     def heads(i, carry):
-        for j in range(UNROLL):
-            head(i * UNROLL + j)
-        after(i * UNROLL + UNROLL - 1)
+        head(2 * i, 0, softmax_of(2 * i + 1, 1))
+        head(2 * i + 1, 1, softmax_of(2 * i + 2, 0))
+        after(2 * i + 1)
         return carry
 
-    lax.fori_loop(0, HEADS // UNROLL, heads, 0)
+    lax.fori_loop(0, HEADS // 2 - 1, heads, 0)
+    head(HEADS - 2, 0, softmax_of(HEADS - 1, 1))
+    head(HEADS - 1, 1, lambda b: None)
 
 
 def layer_kernel(
@@ -154,7 +185,7 @@
     code_ref, mixed_ref, local_ref, ret_ref, sums_ref, tails_ref,
     send, got, flat, back_send, back_got,
     hil, qkv, up, normed, low, low_rows, att, gqkv, chunk,
-    half_send, half_got, piece_send, piece_got, done, pair_send, pair_got,
+    half_send, half_got, piece_send, piece_got, done, pair_send, pair_got, expo,
     go_sems, back_sems, half_sems, piece_sems, done_sems, last_sems, pair_sems, tail_sems,
 ):
     greet()
@@ -222,7 +253,8 @@
 
     def gradients(first, wide):
         parts = [gqkv[pl.ds(m * C + first, wide), :] for m in range(3)]
-        sums = [jnp.dot(part, low_rows[...], preferred_element_type=F) for part in parts]
+        sums = jnp.dot(jnp.concatenate(parts, 0), low_rows[...], preferred_element_type=F)
+        sums = [sums[m * wide : (m + 1) * wide] for m in range(3)]
         span = pl.ds(first, wide)
         return sums + [jnp.dot(att[span, :], d_mixed_ref[...], preferred_element_type=F)]
 
@@ -242,16 +274,16 @@
         piece_send[...] = (kept + half_got[...].astype(F)).astype(B)
         piece_got[own, :] = piece_send[own, :]
 
-        def scatter(step, carry):
+        def scatter(step):
             to = lax.rem(chip + step, CHIPS)
             theirs = pl.ds(pl.multiple_of(to * PIECE, PIECE), PIECE)
             remote(
                 piece_send.at[theirs], piece_got.at[own],
                 piece_sems.at[0], piece_sems.at[1], to * 2 + core,
             ).start()
-            return carry
-
-        lax.fori_loop(1, CHIPS, scatter, 0)
+
+        for step in range(1, CHIPS):
+            scatter(step)
 
     def total_of(pieces, count):
         total = pieces[0:PIECE, :].astype(F)
@@ -263,14 +295,14 @@
         await_bytes(piece_got.at[others], piece_sems.at[1])
         done[own, :] = total_of(piece_got, CHIPS)
 
-        def gather(step, carry):
+        def gather(step):
             to = lax.rem(chip + step, CHIPS)
             remote(
                 done.at[own], done.at[own], done_sems.at[0], done_sems.at[1], to * 2 + core
             ).start()
-            return carry
-
-        lax.fori_loop(1, CHIPS, gather, 0)
+
+        for step in range(1, CHIPS):
+            gather(step)
 
     def share_sum():
         await_bytes(done.at[others], done_sems.at[1])
@@ -288,7 +320,7 @@
     turn = lax.rem(me, PAIRS)
 
     def start_pair(c):
-        sums = gradients(pl.multiple_of(WIDE + c * PAIR, PAIR), PAIR)
+        sums = gradients(WIDE + c * PAIR if isinstance(c, int) else pl.multiple_of(WIDE + c * PAIR, PAIR), PAIR)
         for m in range(4):
             for side in range(2):
                 first = (side * 4 + m) * PAIR
@@ -299,12 +331,11 @@
         def piece(m):
             return pair_send.at[c, pl.ds(pl.multiple_of(m * PIECE, PIECE), PIECE)]
 
-        def scatter(step, carry):
+        def scatter(step):
             m = lax.rem(me // PAIRS + step, OWNERS)
             remote(
                 piece(m), pair_got.at[mine], pair_sems.at[0], pair_sems.at[1], m * PAIRS + c
             ).start()
-            return carry
 
         @pl.when(turn == c)
         def _():
@@ -312,37 +343,38 @@
 
         @pl.when(turn != c)
         def _():
-            scatter(0, 0)
-
-        lax.fori_loop(1, OWNERS, scatter, 0)
+            scatter(0)
+
+        for step in range(1, OWNERS):
+            scatter(step)
 
     def finish_pair():
         await_bytes(pair_got.at[peers], pair_sems.at[1])
         tails_ref[mine, :] = total_of(pair_got, PEERS)
 
-        def gather(step, carry):
+        def gather(step):
             peer = lax.rem(me + step, PEERS)
             remote(
                 tails_ref.at[mine], tails_ref.at[mine], tail_sems.at[0], tail_sems.at[1], peer
             ).start()
-            return carry
-
-        lax.fori_loop(1, PEERS, gather, 0)
+
+        for step in range(1, PEERS):
+            gather(step)
 
     def after(h):
         for k, stage in enumerate((start_sum, scatter_sum, gather_sum, share_sum)):
             pl.when(h == HEADS // 2 - 1 + 2 * k)(stage)
         first = HEADS // 2 + 1
-        for c in range(2):
-            pl.when((h == first + 2 * c + 4) & (turn == c))(finish_pair)
         pl.when(h >= first)(lambda: start_pair((h - first) // 2))
 
     patch = patch_ref[...]
     attention(
         qkv.at[:C], qkv.at[C : 2 * C], qkv.at[2 * C :], up,
         (patch == patch[:, :1]).astype(F),
-        att, gqkv.at[:C], gqkv.at[C : 2 * C], gqkv.at[2 * C :], after,
+        att, gqkv.at[:C], gqkv.at[C : 2 * C], gqkv.at[2 * C :], expo, after,
     )
+
+    start_pair(PAIRS - 1)
 
     grad_normed = jnp.dot(w_qkv_ref[...], gqkv[...], preferred_element_type=F)
     scaled = grad_normed * gain
@@ -357,7 +389,7 @@
     for o in range(PEERS):
         back_send[o] = back[o * CAP : (o + 1) * CAP].astype(B)
     exchange(back_send, back_got, back_sems.at[0], back_sems.at[1])
-    pl.when(turn >= 2)(finish_pair)
+    finish_pair()
     stay = (p == here).astype(F).astype(B)
     local_ref[...] = jnp.dot(d_rows, stay, preferred_element_type=F).astype(B)
     mixed_ref[...] = (hil[...].astype(F) + dg(att[...], w_out_ref[...], 0, 0)).astype(B)
@@ -372,9 +404,11 @@
 
 
 def finish_kernel(
-    code_ref, ret_ref, local_ref, sums_ref, tails_ref, w_qkv_ref, gain_ref,
-    d_feats_ref, g_qkv_ref, g_out_ref, g_gain_ref,
+    code_ref, ret_ref, local_ref, sums_ref, tails_ref, w_qkv_ref, gain_ref, rows_ref,
+    d_feats_ref, g_qkv_ref, g_out_ref, g_gain_ref, mixed_ref, sem,
 ):
+    copy = pltpu.make_async_copy(rows_ref, mixed_ref, sem)
+    copy.start()
     d_feats = dg(ret_ref[...], slot_rows(code_ref[...]), 0, 0) + local_ref[...].astype(F)
     d_feats_ref[...] = d_feats.T.astype(B)
 
@@ -402,17 +436,19 @@
                     g_out_ref[g * WIDE : (g + 1) * WIDE, lanes] = part
         total_row = jnp.sum(column.T, axis=0, keepdims=True)
         g_gain_ref[:, lanes] = total_row / gain_ref[:, lanes]
-
-
-def call(kernel, out_shapes, n_in, scratch=(), collective_id=None):
+    copy.wait()
+
+
+def call(kernel, out_shapes, n_in, scratch=(), collective_id=None, through=0):
     params = dict(vmem_limit_bytes=VMEM)
     if collective_id is not None:
         params.update(collective_id=collective_id, has_side_effects=True)
     return pl.pallas_call(
         kernel,
         out_shape=[jax.ShapeDtypeStruct(s, d) for s, d in out_shapes],
-        in_specs=[ANYWHERE] * n_in,
-        out_specs=[ANYWHERE] * len(out_shapes),
+        in_specs=[VECTOR] * (n_in - through) + [pl.BlockSpec(memory_space=pl.ANY)] * through,
+        out_specs=[VECTOR] * (len(out_shapes) - through)
+        + [pl.BlockSpec(memory_space=pl.ANY)] * through,
         scratch_shapes=list(scratch),
         compiler_params=pltpu.CompilerParams(**params),
     )
@@ -439,12 +475,17 @@
         ]
         + [pltpu.VMEM(half, B)] * 5
         + [pltpu.VMEM((PAIRS, OWNERS * PIECE, 128), B), pltpu.VMEM(whole, B)]
+        + [pltpu.VMEM((2, N, N), B)]
         + [dma((2,))] * 8,
         collective_id=0,
     )(rank, feats, patch, gain, w_qkv, w_out, d_mixed)
-    d_feats, g_qkv, g_out, g_gain = call(
-        finish_kernel, [((N, C), B), ((C, 3 * C), F), ((C, C), F), ((1, C), F)], 7
-    )(code, ret, local, sums, tails, w_qkv, gain)
+    d_feats, g_qkv, g_out, g_gain, mixed = call(
+        finish_kernel,
+        [(by_point, B), ((C, 3 * C), F), ((C, C), F), ((1, C), F), (by_point, B)],
+        8,
+        [dma],
+        through=1,
+    )(code, ret, local, sums, tails, w_qkv, gain, mixed)
     return (mixed, d_feats, g_qkv, g_out, g_gain.reshape(C))
 
 

time: 84.9 us -> 98.6 us (1.16)
  Pallas kernels: 83.3 us -> 97.6 us
    pallas_call x1, Pallas kernels: 3.03 us -> 19.5 us  [on_device(): call(finish_kernel, [(by_point, B), ((C, 3 * C), F), ((C, C), F), ((1, C)...]
    pallas_call x1, Pallas kernels: 80.3 us -> 78.1 us  [on_device(): call(layer_kernel, [((1, N), I), (by_point, B), (by_channel, B), ((SLOTS,...]
where the time goes in v5:
time: 98.6 us; the launch traced here: 98.4 us
  Pallas kernels  97.6 us (99%)
    pallas_call x1, Pallas kernels, on_device(): call(layer_kernel, [((1, N), I), (by_point, B), (by_channel, B), ((SLOTS,...  78.1 us
    pallas_call x1, Pallas kernels, on_device(): call(finish_kernel, [(by_point, B), ((C, 3 * C), F), ((C, C), F), ((1, C)...  19.5 us

profile of v5, /device:TPU:1, one launch (start us, length us, event | category | flops | bytes accessed | tf_op | source)
XLA Modules:
  0.0 98.4 jit_solution(13999118246596216746)
XLA Ops:
  0.6 78.1 %shard_map.110 = (s32[1,1024]{1,0:T(1,128)}, bf16[1024,256]{1,0:T(8,128)(2,1)}, bf16[256,1024]{1,0:T(8,128)(2,1)}, bf16[256,256]{1,0:T(8,128)(2,1)}, bf16[1024,1...) custom-call(s32[1,1024]{1,0:T(1,128)} %bitcast.4, bf16[1024,256]{1,0:T(8,128)(2,1)} %feats_ref.1, s32[1,1024]{1,0:T(1,128)} %bitcast.5, ...), custom_call_target="tpu_custom_call" | custom-call | tf_op jit(solution)/shard_map/pallas_call | solution.py:465
  78.7 19.5 %shard_map.111 = (bf16[1024,256]{1,0:T(8,128)(2,1)}, f32[256,768]{1,0:T(8,128)}, f32[256,256]{1,0:T(8,128)}, f32[1,256]{1,0:T(1,128)}, bf16[1024,256]{1,0:T(8,128)(2,1)}) custom-call(s32[1,1024]{1,0:T(1,128)} %get-tuple-element.16.code_ref, bf16[256,256]{1,0:T(8,128)(2,1)} %get-tuple-element.17.ret_ref, bf16[256,1024]{1,0:T(8,128)(2,1)} %get-tuple-element.18.local_ref, ...), custom_call_target="tpu_custom_call" | custom-call | tf_op jit(solution)/shard_map/pallas_call | solution.py:482

commit v6 on v5

--- a/solution.py
+++ b/solution.py
@@ -405,10 +405,9 @@
 
 def finish_kernel(
     code_ref, ret_ref, local_ref, sums_ref, tails_ref, w_qkv_ref, gain_ref, rows_ref,
-    d_feats_ref, g_qkv_ref, g_out_ref, g_gain_ref, mixed_ref, sem,
+    d_feats_ref, g_qkv_ref, g_out_ref, g_gain_ref, mixed_ref,
 ):
-    copy = pltpu.make_async_copy(rows_ref, mixed_ref, sem)
-    copy.start()
+    mixed_ref[...] = rows_ref[...]
     d_feats = dg(ret_ref[...], slot_rows(code_ref[...]), 0, 0) + local_ref[...].astype(F)
     d_feats_ref[...] = d_feats.T.astype(B)
 
@@ -436,19 +435,17 @@
                     g_out_ref[g * WIDE : (g + 1) * WIDE, lanes] = part
         total_row = jnp.sum(column.T, axis=0, keepdims=True)
         g_gain_ref[:, lanes] = total_row / gain_ref[:, lanes]
-    copy.wait()
-
-
-def call(kernel, out_shapes, n_in, scratch=(), collective_id=None, through=0):
+
+
+def call(kernel, out_shapes, n_in, scratch=(), collective_id=None):
     params = dict(vmem_limit_bytes=VMEM)
     if collective_id is not None:
         params.update(collective_id=collective_id, has_side_effects=True)
     return pl.pallas_call(
         kernel,
         out_shape=[jax.ShapeDtypeStruct(s, d) for s, d in out_shapes],
-        in_specs=[VECTOR] * (n_in - through) + [pl.BlockSpec(memory_space=pl.ANY)] * through,
-        out_specs=[VECTOR] * (len(out_shapes) - through)
-        + [pl.BlockSpec(memory_space=pl.ANY)] * through,
+        in_specs=[VECTOR] * n_in,
+        out_specs=[VECTOR] * len(out_shapes),
         scratch_shapes=list(scratch),
         compiler_params=pltpu.CompilerParams(**params),
     )
@@ -483,8 +480,6 @@
         finish_kernel,
         [(by_point, B), ((C, 3 * C), F), ((C, C), F), ((1, C), F), (by_point, B)],
         8,
-        [dma],
-        through=1,
     )(code, ret, local, sums, tails, w_qkv, gain, mixed)
     return (mixed, d_feats, g_qkv, g_out, g_gain.reshape(C))
 

time: 98.6 us -> 82.2 us (0.83)
  Pallas kernels: 97.6 us -> 81.5 us
    pallas_call x1, Pallas kernels: 19.5 us -> 3.36 us  [on_device(): call(finish_kernel, [(by_point, B), ((C, 3 * C), F), ((C, C), F), ((1, C)...]
where the time goes in v6:
time: 82.2 us; the launch traced here: 82.1 us
  Pallas kernels  81.5 us (99%)
    pallas_call x1, Pallas kernels, on_device(): call(layer_kernel, [((1, N), I), (by_point, B), (by_channel, B), ((SLOTS,...  78.1 us
    pallas_call x1, Pallas kernels, on_device(): call(finish_kernel, [(by_point, B), ((C, 3 * C), F), ((C, C), F), ((1, C)...  3.36 us

profile of v6, /device:TPU:1, one launch (start us, length us, event | category | flops | bytes accessed | tf_op | source)
XLA Modules:
  0.0 82.1 jit_solution(1119077130785872115)
XLA Ops:
  0.6 78.1 %shard_map.110 = (s32[1,1024]{1,0:T(1,128)}, bf16[1024,256]{1,0:T(8,128)(2,1)}, bf16[256,1024]{1,0:T(8,128)(2,1)}, bf16[256,256]{1,0:T(8,128)(2,1)}, bf16[1024,1...) custom-call(s32[1,1024]{1,0:T(1,128)} %bitcast.4, bf16[1024,256]{1,0:T(8,128)(2,1)} %feats_ref.1, s32[1,1024]{1,0:T(1,128)} %bitcast.5, ...), custom_call_target="tpu_custom_call" | custom-call | tf_op jit(solution)/shard_map/pallas_call | solution.py:462
  78.7 3.4 %shard_map.111 = (bf16[1024,256]{1,0:T(8,128)(2,1)}, f32[256,768]{1,0:T(8,128)}, f32[256,256]{1,0:T(8,128)}, f32[1,256]{1,0:T(1,128)}, bf16[1024,256]{1,0:T(8,128)(2,1)}) custom-call(s32[1,1024]{1,0:T(1,128)} %get-tuple-element.16.code_ref, bf16[256,256]{1,0:T(8,128)(2,1)} %get-tuple-element.17.ret_ref, bf16[256,1024]{1,0:T(8,128)(2,1)} %get-tuple-element.18.local_ref, ...), custom_call_target="tpu_custom_call" | custom-call | tf_op jit(solution)/shard_map/pallas_call | solution.py:479

commit v7 on v6

--- a/solution.py
+++ b/solution.py
@@ -185,7 +185,7 @@
     code_ref, mixed_ref, local_ref, ret_ref, sums_ref, tails_ref,
     send, got, flat, back_send, back_got,
     hil, qkv, up, normed, low, low_rows, att, gqkv, chunk,
-    half_send, half_got, piece_send, piece_got, done, pair_send, pair_got, expo,
+    half_send, half_got, piece_send, piece_got, done, pair_send, pair_got, expo, d_mixed, come,
     go_sems, back_sems, half_sems, piece_sems, done_sems, last_sems, pair_sems, tail_sems,
 ):
     greet()
@@ -226,6 +226,7 @@
     hil[...] = jnp.dot(stay, feats_ref[...], preferred_element_type=F).astype(B)
     up[...] = dg(w_out_ref[...], d_mixed_ref[...], 1, 1).astype(B)
     gain = jnp.broadcast_to(gain_ref[...], (8, C)).T[:, :1]
+    d_mixed[...] = d_mixed_ref[...].T
     await_exchange(got, go_sems.at[1])
     await_exchange(send, go_sems.at[0])
 
@@ -237,9 +238,9 @@
     valid = jnp.where(iota((16, 128), 1) == 2, 1.0, 0.0).astype(B)
     at = dg(weight, spots, 1, 1)[:1]
     at = jnp.where(dg(valid, spots, 1, 1)[:1] > 0.5, at, -1.0).astype(I)
-    come = (p == at).astype(F).astype(B)
+    come[...] = (p == at).astype(F).astype(B)
     rows = hil[...].astype(F)
-    rows += jnp.dot(come, flat[:, :C].astype(B), preferred_element_type=F)
+    rows += jnp.dot(come[...], flat[:, :C].astype(B), preferred_element_type=F)
     hil[...] = rows.astype(B)
 
     wide = rows.T
@@ -383,15 +384,14 @@
         - jnp.mean(scaled, axis=0, keepdims=True)
         - normed[...] * jnp.mean(scaled * normed[...], axis=0, keepdims=True)
     )
-    d_rows = (d_mixed_ref[...].astype(F).T + d_norm).astype(B)
-    come = (p == at).astype(F).astype(B)
-    back = jnp.dot(d_rows, come, preferred_element_type=F).T
+    d_rows = (d_mixed[...].astype(F) + d_norm).astype(B)
+    back = jnp.dot(d_rows, come[...], preferred_element_type=F).T
     for o in range(PEERS):
         back_send[o] = back[o * CAP : (o + 1) * CAP].astype(B)
     exchange(back_send, back_got, back_sems.at[0], back_sems.at[1])
     finish_pair()
     stay = (p == here).astype(F).astype(B)
-    local_ref[...] = jnp.dot(d_rows, stay, preferred_element_type=F).astype(B)
+    local_ref[...] = jnp.dot(d_rows, stay, preferred_element_type=F).T.astype(B)
     mixed_ref[...] = (hil[...].astype(F) + dg(att[...], w_out_ref[...], 0, 0)).astype(B)
     end_sum()
     await_exchange(back_got, back_sems.at[1])
@@ -408,8 +408,8 @@
     d_feats_ref, g_qkv_ref, g_out_ref, g_gain_ref, mixed_ref,
 ):
     mixed_ref[...] = rows_ref[...]
-    d_feats = dg(ret_ref[...], slot_rows(code_ref[...]), 0, 0) + local_ref[...].astype(F)
-    d_feats_ref[...] = d_feats.T.astype(B)
+    d_feats = dg(slot_rows(code_ref[...]), ret_ref[...], 0, 0) + local_ref[...].astype(F)
+    d_feats_ref[...] = d_feats.astype(B)
 
     def sums(m, side):
         first = (m // 2) * HALF + side * 2 * WIDE + (m % 2) * WIDE
@@ -461,7 +461,7 @@
     out_block, back_block = (PEERS, CAP, C + 128), (PEERS, CAP, C)
     code, mixed, local, ret, sums, tails = call(
         layer_kernel,
-        [((1, N), I), (by_point, B), (by_channel, B), ((SLOTS, C), B), (whole, B), (whole, B)],
+        [((1, N), I), (by_point, B), (by_point, B), ((SLOTS, C), B), (whole, B), (whole, B)],
         7,
         [
             pltpu.VMEM(out_block, B), pltpu.VMEM(out_block, B), pltpu.VMEM((SLOTS, C + 128), F),
@@ -472,7 +472,7 @@
         ]
         + [pltpu.VMEM(half, B)] * 5
         + [pltpu.VMEM((PAIRS, OWNERS * PIECE, 128), B), pltpu.VMEM(whole, B)]
-        + [pltpu.VMEM((2, N, N), B)]
+        + [pltpu.VMEM((2, N, N), B), pltpu.VMEM(by_channel, B), pltpu.VMEM(by_point, B)]
         + [dma((2,))] * 8,
         collective_id=0,
     )(rank, feats, patch, gain, w_qkv, w_out, d_mixed)

time: 82.2 us -> 82.3 us (level)
  no operation moved by 1% of the time
where the time goes in v7:
time: 82.3 us; the launch traced here: 82.1 us
  Pallas kernels  81.5 us (99%)
    pallas_call x1, Pallas kernels, on_device(): call(layer_kernel, [((1, N), I), (by_point, B), (by_point, B), ((SLOTS, C...  78.2 us
    pallas_call x1, Pallas kernels, on_device(): call(finish_kernel, [(by_point, B), ((C, 3 * C), F), ((C, C), F), ((1, C)...  3.31 us

profile of v7, /device:TPU:1, one launch (start us, length us, event | category | flops | bytes accessed | tf_op | source)
XLA Modules:
  0.0 82.1 jit_solution(10043541187894646815)
XLA Ops:
  0.6 78.2 %shard_map.110 = (s32[1,1024]{1,0:T(1,128)}, bf16[1024,256]{1,0:T(8,128)(2,1)}, bf16[1024,256]{1,0:T(8,128)(2,1)}, bf16[256,256]{1,0:T(8,128)(2,1)}, bf16[1024,1...) custom-call(s32[1,1024]{1,0:T(1,128)} %bitcast.4, bf16[1024,256]{1,0:T(8,128)(2,1)} %feats_ref.1, s32[1,1024]{1,0:T(1,128)} %bitcast.5, ...), custom_call_target="tpu_custom_call" | custom-call | tf_op jit(solution)/shard_map/pallas_call | solution.py:462
  78.8 3.3 %shard_map.111 = (bf16[1024,256]{1,0:T(8,128)(2,1)}, f32[256,768]{1,0:T(8,128)}, f32[256,256]{1,0:T(8,128)}, f32[1,256]{1,0:T(1,128)}, bf16[1024,256]{1,0:T(8,128)(2,1)}) custom-call(s32[1,1024]{1,0:T(1,128)} %get-tuple-element.16.code_ref, bf16[256,256]{1,0:T(8,128)(2,1)} %get-tuple-element.17.ret_ref, bf16[1024,256]{1,0:T(8,128)(2,1)} %get-tuple-element.18.local_ref, ...), custom_call_target="tpu_custom_call" | custom-call | tf_op jit(solution)/shard_map/pallas_call | solution.py:479
